TPU v7x, 32 devices: a whole 2x2x4 slice. The times are simulated.
32 devices in a mesh: fsdp: 8 (over z, y), seq: 4 (over x, core).
Axes of the slice: x: 2, y: 2, z: 4, core: 2. Of those that a mesh axis runs over, the one named last changes fastest.
Arguments:
- hidden_in: bfloat16 [4096, 768], P(('fsdp', 'seq')), may hold values from -6 to 6
- cu_lengths: int32 [8, 7], P('fsdp'), may hold values from 0 to 512, as said below
- w_qkv: bfloat16 [2, 768, 2304], P(None, 'fsdp'), may hold values from -0.21875 to 0.21875
- w_attn_out: bfloat16 [2, 768, 768], P(None, 'fsdp'), may hold values from -0.875 to 0.875
- w_in: bfloat16 [2, 768, 2304], P(None, 'fsdp'), may hold values from -0.21875 to 0.21875
- w_ff_out: bfloat16 [2, 1152, 768], P(None, 'fsdp'), may hold values from -0.1875 to 0.1875
- gains: bfloat16 [2, 2, 768], P(None, None, 'fsdp'), may hold values from 0.25 to 1.75
- cotangent: bfloat16 [4096, 768], P(('fsdp', 'seq')), may hold values from -6 to 6
Outputs:
- block_out: bfloat16 [4096, 768], P(('fsdp', 'seq'))
- grad_hidden: float32 [4096, 768], P(('fsdp', 'seq'))
- grad_w_qkv: float32 [2, 768, 2304], P(None, 'fsdp')
- grad_w_attn_out: float32 [2, 768, 768], P(None, 'fsdp')
- grad_w_in: float32 [2, 768, 2304], P(None, 'fsdp')
- grad_w_ff_out: float32 [2, 1152, 768], P(None, 'fsdp')
- grad_gains: float32 [2, 2, 768], P(None, None, 'fsdp')
Inputs may be any that keep to these rules, and one draw needn't show every extreme that they name: `cu_lengths`: in every group the entries rise strictly from 0 to 512; one document starts before token 128 and ends after token 384.
All inputs are finite; a program needn't handle non-finite values.
Results may differ from a plain program's by a relative error of at most 0.025.
Values may be sent and summed in bfloat16 or wider, within the bound.
A program may use at most 192 MiB of HBM per device.

v0:
```python
import jax
import jax.numpy as jnp
from jax import lax
from jax.sharding import PartitionSpec as P

D = 768
HEADS = 12
HEAD = 64
FF = 1152
LAYERS = 2
HALF_WINDOW = 64


EPS = 1e-05
NEG = -1e30
LOCAL_BASE = 10000.0
GLOBAL_BASE = 160000.0


def layer_norm(stream, gain):
    mean_row = jnp.mean(stream, axis=-1, keepdims=True)
    centred = stream - mean_row
    spread = jnp.mean(centred * centred, axis=-1, keepdims=True)
    return centred * lax.rsqrt(spread + EPS) * gain


def geglu(lifted):
    half_width = lifted.shape[-1] // 2
    return jax.nn.gelu(lifted[:, :half_width], approximate=False) * lifted[:, half_width:]


def doc_layout(cu_row, group_rows):
    places = jnp.arange(group_rows, dtype=jnp.int32)
    inner_cuts = cu_row[1:-1]
    doc_ids = jnp.sum((places[:, None] >= inner_cuts[None, :]).astype(jnp.int32), axis=1)
    heads_of = cu_row[:-1]
    starts = jnp.max(jnp.where(places[:, None] >= heads_of[None, :], heads_of[None, :], 0), axis=1)
    return (doc_ids, places - starts)


def rope_tables(positions, base_freq):
    freqs = base_freq ** (-jnp.arange(0, HEAD, 2, dtype=jnp.float32) / HEAD)
    angles = positions.astype(jnp.float32)[:, None] * freqs[None, :]
    angles = jnp.concatenate([angles, angles], axis=1)
    return (jnp.cos(angles), jnp.sin(angles))


def rotate(values, cosine, sine_tab):
    half_width = values.shape[-1] // 2
    turned = jnp.concatenate([-values[..., half_width:], values[..., :half_width]], axis=-1)
    return values * cosine[:, None, :] + turned * sine_tab[:, None, :]


def unrotate(gradient, cosine, sine_tab):
    half_width = gradient.shape[-1] // 2
    scaled = gradient * sine_tab[:, None, :]
    turned = jnp.concatenate([scaled[..., half_width:], -scaled[..., :half_width]], axis=-1)
    return gradient * cosine[:, None, :] + turned


def masked_scores(head_rows, allowed):
    score_scale = head_rows.shape[-1] ** (-0.5)
    scores = (
        jnp.einsum(
            "qhd,khd->hqk", head_rows[:, 0], head_rows[:, 1], preferred_element_type=jnp.float32
        )
        * score_scale
    )
    return jnp.where(allowed[None], scores, NEG)


def attend(head_rows, allowed):
    scores = masked_scores(head_rows, allowed)
    row_max = jnp.max(scores, axis=-1, keepdims=True)
    expd = jnp.exp(scores - row_max)
    denom_sum = jnp.sum(expd, axis=-1, keepdims=True)
    attn_probs = (expd / denom_sum).astype(jnp.bfloat16)
    mixture = jnp.einsum(
        "hqk,khd->qhd", attn_probs, head_rows[:, 2], preferred_element_type=jnp.float32
    )
    return (mixture, row_max[..., 0] + jnp.log(denom_sum[..., 0]))


def attend_back(head_rows, allowed, log_total, grad_heads):
    score_scale = head_rows.shape[-1] ** (-0.5)
    scores = masked_scores(head_rows, allowed)
    attn_probs = jnp.exp(scores - log_total[..., None])
    grad_probs = jnp.einsum(
        "qhd,khd->hqk", grad_heads, head_rows[:, 2], preferred_element_type=jnp.float32
    )
    centre = jnp.sum(attn_probs * grad_probs, axis=-1, keepdims=True)
    grad_scores = (attn_probs * (grad_probs - centre)).astype(jnp.bfloat16)
    grad_q = (
        jnp.einsum("hqk,khd->qhd", grad_scores, head_rows[:, 1], preferred_element_type=jnp.float32)
        * score_scale
    )
    grad_k = (
        jnp.einsum("hqk,qhd->khd", grad_scores, head_rows[:, 0], preferred_element_type=jnp.float32)
        * score_scale
    )
    grad_v = jnp.einsum(
        "hqk,qhd->khd",
        attn_probs.astype(jnp.bfloat16),
        grad_heads,
        preferred_element_type=jnp.float32,
    )
    return (grad_q, grad_k, grad_v)


def on_device(hidden_in, cu_lengths, w_qkv, w_attn_out, w_in, w_ff_out, gains, cotangent):
    local_rows = hidden_in.shape[0]
    seq_count = lax.axis_size("seq")
    group_rows = local_rows * seq_count
    part_width = D // seq_count
    part_heads = part_width // HEAD
    doc_ids, positions = doc_layout(cu_lengths[0], group_rows)
    offset = lax.axis_index("seq") * local_rows
    my_pos = lax.dynamic_slice_in_dim(positions, offset, local_rows)
    places = jnp.arange(group_rows, dtype=jnp.int32)
    same_doc = doc_ids[:, None] == doc_ids[None, :]
    distance = jnp.abs(places[:, None] - places[None, :])
    stream = hidden_in.astype(jnp.float32)
    stored = []
    resident = []
    for layer_at in range(LAYERS):
        weights_now = (
            lax.all_gather(w_qkv[layer_at], "fsdp", axis=0, tiled=True),
            lax.all_gather(w_attn_out[layer_at], "fsdp", axis=0, tiled=True),
            lax.all_gather(w_in[layer_at], "fsdp", axis=0, tiled=True),
            lax.all_gather(w_ff_out[layer_at], "fsdp", axis=0, tiled=True),
            lax.all_gather(gains[layer_at], "fsdp", axis=1, tiled=True),
        )
        qkv_full, proj_full, lift_full, down_full, gain_full = weights_now
        reach = HALF_WINDOW if layer_at == 0 else group_rows
        base_freq = LOCAL_BASE if layer_at == 0 else GLOBAL_BASE
        cosine, sine_tab = rope_tables(my_pos, base_freq)
        allowed = same_doc & (distance <= reach)
        entering = stream
        normed = layer_norm(stream, gain_full[0].astype(jnp.float32)).astype(jnp.bfloat16)
        qkv_rows = jnp.dot(normed, qkv_full, preferred_element_type=jnp.float32).reshape(
            local_rows, 3, HEADS, HEAD
        )
        queries = rotate(qkv_rows[:, 0], cosine, sine_tab)
        key_rows = rotate(qkv_rows[:, 1], cosine, sine_tab)
        packed = jnp.stack([queries, key_rows, qkv_rows[:, 2]], axis=1).astype(jnp.bfloat16)
        packed = packed.reshape(local_rows, 3, seq_count, part_width)
        head_rows = lax.all_to_all(packed, "seq", split_axis=2, concat_axis=0, tiled=True).reshape(
            group_rows, 3, part_heads, HEAD
        )
        mixture, log_total = attend(head_rows, allowed)
        mixture = mixture.astype(jnp.bfloat16).reshape(group_rows, part_width)
        returned = lax.all_to_all(mixture, "seq", split_axis=0, concat_axis=1, tiled=True)
        stream = stream + jnp.dot(returned, proj_full, preferred_element_type=jnp.float32)
        middle = stream
        normed_ff = layer_norm(stream, gain_full[1].astype(jnp.float32)).astype(jnp.bfloat16)
        lifted = jnp.dot(normed_ff, lift_full, preferred_element_type=jnp.float32)
        gated_act = geglu(lifted).astype(jnp.bfloat16)
        stream = stream + jnp.dot(gated_act, down_full, preferred_element_type=jnp.float32)
        stored.append(
            (
                entering,
                normed,
                head_rows,
                log_total,
                allowed,
                cosine,
                sine_tab,
                returned,
                middle,
                normed_ff,
                lifted,
                gated_act,
            )
        )
        resident.append(weights_now)
    block_out = stream.astype(jnp.bfloat16)
    gradient = cotangent.astype(jnp.float32)
    grad_parts = [None] * LAYERS
    for layer_at in reversed(range(LAYERS)):
        (
            entering,
            normed,
            head_rows,
            log_total,
            allowed,
            cosine,
            sine_tab,
            returned,
            middle,
            normed_ff,
            lifted,
            gated_act,
        ) = stored[layer_at]
        weights_now = (
            lax.all_gather(w_qkv[layer_at], "fsdp", axis=0, tiled=True),
            lax.all_gather(w_attn_out[layer_at], "fsdp", axis=0, tiled=True),
            lax.all_gather(w_in[layer_at], "fsdp", axis=0, tiled=True),
            lax.all_gather(w_ff_out[layer_at], "fsdp", axis=0, tiled=True),
            lax.all_gather(gains[layer_at], "fsdp", axis=1, tiled=True),
        )
        qkv_full, proj_full, lift_full, down_full, gain_full = weights_now
        gain_attn = gain_full[0].astype(jnp.float32)
        gain_ffn = gain_full[1].astype(jnp.float32)
        grad_down = gradient.astype(jnp.bfloat16)
        grad_gated = jnp.dot(grad_down, down_full.T, preferred_element_type=jnp.float32)
        _, pullback = jax.vjp(geglu, lifted)
        grad_lift = pullback(grad_gated)[0].astype(jnp.bfloat16)
        grad_normed = jnp.dot(grad_lift, lift_full.T, preferred_element_type=jnp.float32)
        _, pullback = jax.vjp(layer_norm, middle, gain_ffn)
        grad_input, grad_gain_ffn = pullback(grad_normed)
        gradient = gradient + grad_input
        grad_proj_out = gradient.astype(jnp.bfloat16)
        grad_mixture = jnp.dot(
            grad_proj_out, proj_full.T, preferred_element_type=jnp.float32
        ).astype(jnp.bfloat16)
        grad_heads = lax.all_to_all(
            grad_mixture, "seq", split_axis=1, concat_axis=0, tiled=True
        ).reshape(group_rows, part_heads, HEAD)
        grad_q, grad_k, grad_v = attend_back(head_rows, allowed, log_total, grad_heads)
        grad_stack = (
            jnp.stack([grad_q, grad_k, grad_v], axis=1)
            .astype(jnp.bfloat16)
            .reshape(group_rows, 3, 1, part_width)
        )
        grad_rows = (
            lax.all_to_all(grad_stack, "seq", split_axis=0, concat_axis=2, tiled=True)
            .reshape(local_rows, 3, HEADS, HEAD)
            .astype(jnp.float32)
        )
        grad_qkv = jnp.stack(
            [
                unrotate(grad_rows[:, 0], cosine, sine_tab),
                unrotate(grad_rows[:, 1], cosine, sine_tab),
                grad_rows[:, 2],
            ],
            axis=1,
        )
        grad_qkv = grad_qkv.reshape(local_rows, 3 * HEADS * HEAD).astype(jnp.bfloat16)
        grad_normed = jnp.dot(grad_qkv, qkv_full.T, preferred_element_type=jnp.float32)
        _, pullback = jax.vjp(layer_norm, entering, gain_attn)
        grad_input, grad_gain_attn = pullback(grad_normed)
        gradient = gradient + grad_input
        gain_grads = jnp.stack([grad_gain_attn, grad_gain_ffn])
        gain_cols = gain_grads.T
        model_share = lax.psum_scatter(
            jnp.concatenate(
                [
                    jnp.dot(normed.T, grad_qkv, preferred_element_type=jnp.float32),
                    jnp.dot(returned.T, grad_proj_out, preferred_element_type=jnp.float32),
                    jnp.dot(normed_ff.T, grad_lift, preferred_element_type=jnp.float32),
                    gain_cols,
                ],
                axis=1,
            ),
            "fsdp",
            scatter_dimension=0,
            tiled=True,
        )
        hidden_share = lax.psum_scatter(
            jnp.dot(gated_act.T, grad_down, preferred_element_type=jnp.float32),
            "fsdp",
            scatter_dimension=0,
            tiled=True,
        )
        model_share, hidden_share = (
            lax.psum(model_share.astype(jnp.bfloat16), "seq").astype(jnp.float32),
            lax.psum(hidden_share.astype(jnp.bfloat16), "seq").astype(jnp.float32),
        )
        grad_parts[layer_at] = (
            model_share[:, : 3 * D],
            model_share[:, 3 * D : 4 * D],
            model_share[:, 4 * D : 4 * D + 2 * FF],
            hidden_share,
            model_share[:, 4 * D + 2 * FF :].T,
        )
    stacked = [
        jnp.stack([grad_parts[layer_at][member] for layer_at in range(LAYERS)])
        for member in range(5)
    ]
    return (block_out, gradient, stacked[0], stacked[1], stacked[2], stacked[3], stacked[4])


def solution(mesh):
    return jax.shard_map(
        on_device,
        mesh=mesh,
        in_specs=(
            P(("fsdp", "seq"), None),
            P("fsdp", None),
            P(None, "fsdp", None),
            P(None, "fsdp", None),
            P(None, "fsdp", None),
            P(None, "fsdp", None),
            P(None, None, "fsdp"),
            P(("fsdp", "seq"), None),
        ),
        out_specs=(
            P(("fsdp", "seq"), None),
            P(("fsdp", "seq"), None),
            P(None, "fsdp", None),
            P(None, "fsdp", None),
            P(None, "fsdp", None),
            P(None, "fsdp", None),
            P(None, None, "fsdp"),
        ),
        check_vma=False,
    )
```

profile of v0, /device:TPU:0, one launch (start us, length us, event | category | flops | bytes accessed | tf_op | source)
XLA Modules:
  0.0 1289.5 jit_solution(9966666311263803553)
XLA Ops:
  16.0 34.0 %all-gather = bf16[1,2,768]{1,0,2:T(2,128)(2,1)S(1)} all-gather(bf16[1,2,96]{1,0,2:T(2,128)(2,1)S(1)} %copy.226), channel_id=2, replica_groups=mesh['fsdp'=8,'seq'=4] {'fsdp'}, dimensions={2}, use_global_device_ids=true | all-gather | bytes 3456 | tf_op jit(solution)/shard_map/all_gather | solution.py:131
  50.0 4.6 fusion.99
  56.5 24.8 %all-gather.19.cloned.1.call-done = bf16[1,768,2304]{2,1,0:T(8,128)(2,1)} async-done(((bf16[1,96,2304]{2,1,0:T(8,128)(2,1)}), bf16[1,768,2304]{2,1,0:T(8,128)(2,1)}) %all-gather.19.cloned.1.call-update) | async-done | bytes 3538960 | tf_op jit(solution)/shard_map/all_gather | solution.py:127
  81.3 3.6 fusion.14
  89.9 31.4 %all-gather.5 = bf16[1,2,768]{1,0,2:T(2,128)(2,1)S(1)} all-gather(bf16[1,2,96]{1,0,2:T(2,128)(2,1)S(1)} %copy.227), channel_id=7, replica_groups=mesh['fsdp'=8,'seq'=4] {'fsdp'}, dimensions={2}, use_global_device_ids=true | all-gather | bytes 3456 | tf_op jit(solution)/shard_map/all_gather | solution.py:131
  132.7 4.5 all-to-all-start.1
  137.2 4.6 fusion.97
  147.1 46.1 %all-gather.23.cloned.1.call-done = bf16[1,768,2304]{2,1,0:T(8,128)(2,1)} async-done(((bf16[1,96,2304]{2,1,0:T(8,128)(2,1)}), bf16[1,768,2304]{2,1,0:T(8,128)(2,1)}) %all-gather.23.cloned.1.call-update) | async-done | bytes 3538960 | tf_op jit(solution)/shard_map/all_gather | solution.py:129
  199.1 40.6 %all-gather.25.cloned.1.call-done = bf16[1,1152,768]{2,1,0:T(8,128)(2,1)} async-done(((bf16[1,144,768]{2,1,0:T(8,128)(2,1)}), bf16[1,1152,768]{2,1,0:T(8,128)(2,1)}) %all-gather.25.cloned.1.call-update) | async-done | bytes 1769488 | tf_op jit(solution)/shard_map/all_gather | solution.py:130
  243.7 62.8 %all-gather.27.cloned.1.call-done = bf16[1,768,2304]{2,1,0:T(8,128)(2,1)} async-done(((bf16[1,96,2304]{2,1,0:T(8,128)(2,1)}), bf16[1,768,2304]{2,1,0:T(8,128)(2,1)}) %all-gather.27.cloned.1.call-update) | async-done | bytes 3538960 | tf_op jit(solution)/shard_map/all_gather | solution.py:127
  306.5 3.7 fusion.6
  310.8 12.1 all_to_all.118
  336.4 11.8 all-gather.29.cloned.1.call-done
  352.5 61.8 %all-gather.31.cloned.1.call-done = bf16[1,768,2304]{2,1,0:T(8,128)(2,1)} async-done(((bf16[1,96,2304]{2,1,0:T(8,128)(2,1)}), bf16[1,768,2304]{2,1,0:T(8,128)(2,1)}) %all-gather.31.cloned.1.call-update) | async-done | bytes 3538960 | tf_op jit(solution)/shard_map/all_gather | solution.py:129
  414.3 3.7 fusion.2
  418.0 42.9 %all-gather.33.cloned.1.call-done = bf16[1,1152,768]{2,1,0:T(8,128)(2,1)} async-done(((bf16[1,144,768]{2,1,0:T(8,128)(2,1)}), bf16[1,1152,768]{2,1,0:T(8,128)(2,1)}) %all-gather.33.cloned.1.call-update) | async-done | bytes 1769488 | tf_op jit(solution)/shard_map/all_gather | solution.py:130
  460.9 4.1 fusion.122
  469.5 4.5 multiply_reduce_fusion.2
  478.8 4.0 all-to-all-start.4
  484.1 4.0 all-to-all-done.4
  513.9 17.8 %all_to_all.119 = bf16[512,3,1,192]{3,1,2,0:T(4,128)(2,1)} all-to-all(bf16[512,3,1,192]{3,1,2,0:T(4,128)(2,1)S(1)} %pad_maximum_fusion.4), channel_id=1, replica_groups=mesh['fsdp'=8,'seq'=4] {'seq'}, dimensions={0} | all-to-all | bytes 1179648 | tf_op jit(solution)/shard_map/all_to_all | solution.py:226
  549.3 4.7 fusion.132
  560.5 6.2 pad_maximum_fusion.1
  576.2 4.2 all-to-all-start.6
  581.1 4.7 all-to-all-done.6
  604.6 3.7 all-to-all-start.7
  611.2 4.0 fusion.133
  615.2 7.4 all-to-all-done.7
  633.1 6.1 pad_maximum_fusion
  642.9 276.7 %reduce-scatter.7.cloned.1.call-done = f32[96,5378]{1,0:T(8,128)} async-done(((f32[768,5378]{1,0:T(8,128)}), f32[96,5378]{1,0:T(8,128)}) %reduce-scatter.7.cloned.1.call-update) | async-done | bytes 2065168 | tf_op jit(solution)/shard_map/reduce_scatter | solution.py:245
  922.3 287.1 %reduce-scatter.5.cloned.1.call-done = f32[96,5378]{1,0:T(8,128)} async-done(((f32[768,5378]{1,0:T(8,128)}), f32[96,5378]{1,0:T(8,128)}) %reduce-scatter.5.cloned.1.call-update) | async-done | bytes 2065168 | tf_op jit(solution)/shard_map/reduce_scatter | solution.py:245
  1214.2 56.8 %all-reduce.7.cloned.1.call-done = (bf16[96,5378]{1,0:T(8,128)(2,1)}, bf16[96,5378]{1,0:T(8,128)(2,1)}, bf16[1,144,768]{2,1,0:T(8,128)(2,1)}, bf16[1,144,768]{2,1,0:T(8,128)(2,1)}) async-done(((bf16[96,5378]{1,0:T(8,128)(2,1)}, bf16[96,5378]{1,0:T(8,128)(2,1)}, bf16[1,144,768]{2,1,0:T(8,128)(2,1)}, bf16[1,144,768]{2,1,0:T(8,128)(2,1)}), (bf16[96,5378]{1,0:T(8,128)(2,1)}, bf16[96,5378]{1,0:T(8,128)(2,1)}, ...) | async-done | bytes 2507536 | tf_op jit(solution)/shard_map/psum | solution.py:266
  (401 shorter events, 184.5 us)
Async XLA Ops:
  7.2 74.1 %all-gather.19.cloned.1.call-start = ((), (), s32[]{:S(2)}) async-start(), calls=%async_computation.16 | async-start | bytes 3981312 | tf_op jit(solution)/shard_map/all_gather | solution.py:127
  9.5 133.9 %all-gather.21.cloned.1.call-start = ((), (), s32[]{:S(2)}) async-start(), calls=%async_computation.17 | async-start | bytes 1327104 | tf_op jit(solution)/shard_map/all_gather | solution.py:128
  11.2 43.4 %copy-start.6 = (bf16[128,768]{1,0:T(8,128)(2,1)S(1)}, bf16[128,768]{1,0:T(8,128)(2,1)}, u32[]{:S(2)}) copy-start(bf16[128,768]{1,0:T(8,128)(2,1)} %param.8) | copy-start | bytes 589828
  11.3 44.3 %copy-start.98 = (s32[1,7]{1,0:T(1,128)S(1)}, s32[1,7]{1,0:T(1,128)}, u32[]{:S(2)}) copy-start(s32[1,7]{1,0:T(1,128)} %param.9) | copy-start | bytes 88
  11.3 181.9 %all-gather.23.cloned.1.call-start = ((), (), s32[]{:S(2)}) async-start(), calls=%async_computation.18 | async-start | bytes 3981312 | tf_op jit(solution)/shard_map/all_gather | solution.py:129
  12.3 227.4 %all-gather.25.cloned.1.call-start = ((), (), s32[]{:S(2)}) async-start(), calls=%async_computation.19 | async-start | bytes 1990656 | tf_op jit(solution)/shard_map/all_gather | solution.py:130
  13.2 293.3 %all-gather.27.cloned.1.call-start = ((), (), s32[]{:S(2)}) async-start(), calls=%async_computation.20 | async-start | bytes 3981312 | tf_op jit(solution)/shard_map/all_gather | solution.py:127
  13.8 334.3 %all-gather.29.cloned.1.call-start = ((), (), s32[]{:S(2)}) async-start(), calls=%async_computation.21 | async-start | bytes 1327104 | tf_op jit(solution)/shard_map/all_gather | solution.py:128
  14.4 399.9 %all-gather.31.cloned.1.call-start = ((), (), s32[]{:S(2)}) async-start(), calls=%async_computation.22 | async-start | bytes 3981312 | tf_op jit(solution)/shard_map/all_gather | solution.py:129
  15.1 445.8 %all-gather.33.cloned.1.call-start = ((), (), s32[]{:S(2)}) async-start(), calls=%async_computation.23 | async-start | bytes 1990656 | tf_op jit(solution)/shard_map/all_gather | solution.py:130
  54.8 30.2 %copy-start.69 = (f32[128]{0:T(128)}, f32[128]{0:T(128)S(1)}, u32[]{:S(2)}) copy-start(f32[128]{0:T(128)S(1)} %broadcast_multiply_fusion.5) | copy-start | bytes 1540
  55.6 29.4 %copy-start.85 = (f32[128]{0:T(128)}, f32[128]{0:T(128)S(1)}, u32[]{:S(2)}) copy-start(f32[128]{0:T(128)S(1)} %fusion.139) | copy-start | bytes 1540
  56.5 28.6 %copy-start.53 = (f32[128,64]{0,1:T(8,128)}, f32[128,64]{0,1:T(8,128)S(1)}, u32[]{:S(2)}) copy-start(f32[128,64]{0,1:T(8,128)S(1)} %get-tuple-element.104) | copy-start | bytes 98308
  56.5 28.6 %copy-start.57 = (f32[128,64]{0,1:T(8,128)}, f32[128,64]{0,1:T(8,128)S(1)}, u32[]{:S(2)}) copy-start(f32[128,64]{0,1:T(8,128)S(1)} %get-tuple-element.105) | copy-start | bytes 98308
  86.2 36.4 %all-to-all-start = ((bf16[128,3,4,192]{0,3,1,2:T(8,128)(2,1)}), bf16[128,3,4,192]{0,3,1,2:T(8,128)(2,1)S(1)}, u32[]{:S(2)}, u32[]{:S(2)}) async-start(bf16[128,3,4,192]{0,3,1,2:T(8,128)(2,1)} %copy.176), calls=%async_computation | async-start | bytes 1179648 | tf_op jit(solution)/shard_map/all_to_all | solution.py:147
  132.7 10.7 all-to-all-start.1
  145.2 94.5 %copy-start.3 = (f32[128,768]{1,0:T(8,128)}, f32[128,768]{1,0:T(8,128)S(1)}, u32[]{:S(2)}) copy-start(f32[128,768]{1,0:T(8,128)S(1)} %get-tuple-element.115) | copy-start | bytes 1179652
  242.5 67.8 %copy-start.74 = (f32[128]{0:T(128)}, f32[128]{0:T(128)S(1)}, u32[]{:S(2)}) copy-start(f32[128]{0:T(128)S(1)} %broadcast_multiply_fusion.3) | copy-start | bytes 1540
  243.6 62.9 %copy-start.94 = (f32[128]{0:T(128)}, f32[128]{0:T(128)S(1)}, u32[]{:S(2)}) copy-start(f32[128]{0:T(128)S(1)} %multiply_reduce_fusion.9) | copy-start | bytes 1540
  243.7 66.6 %copy-start.82 = (f32[128]{0:T(128)}, f32[128]{0:T(128)S(1)}, u32[]{:S(2)}) copy-start(f32[128]{0:T(128)S(1)} %fusion.141) | copy-start | bytes 1540
  310.6 15.8 %copy-start.61 = (pred[512,512]{0,1:T(8,128)(4,1)S(1)}, pred[512,512]{0,1:T(8,128)(4,1)}, u32[]{:S(2)}) copy-start(pred[512,512]{0,1:T(8,128)(4,1)} %get-tuple-element.106) | copy-start | bytes 786436
  332.8 15.4 %all-to-all-start.3 = ((bf16[4,128,192]{1,2,0:T(8,128)(2,1)}), bf16[4,128,192]{1,2,0:T(8,128)(2,1)S(1)}, u32[]{:S(2)}, u32[]{:S(2)}) async-start(bf16[4,128,192]{1,2,0:T(8,128)(2,1)} %copy.185), calls=%async_computation.3 | async-start | bytes 393216 | tf_op jit(solution)/shard_map/all_to_all | solution.py:152
  336.1 303.2 %reduce-scatter.11.cloned.1.call-start = ((), (), s32[]{:S(2)}) async-start(), calls=%async_computation.15 | async-start | bytes 3981312 | tf_op jit(solution)/shard_map/reduce_scatter | solution.py:259
  478.8 9.4 all-to-all-start.4
  482.8 158.4 %reduce-scatter.9.cloned.1.call-start = ((), (), s32[]{:S(2)}) async-start(), calls=%async_computation.14 | async-start | bytes 3981312 | tf_op jit(solution)/shard_map/reduce_scatter | solution.py:259
  545.5 374.1 %reduce-scatter.7.cloned.1.call-start = ((), (), s32[]{:S(2)}) async-start(), calls=%async_computation.13 | async-start | bytes 19021824 | tf_op jit(solution)/shard_map/reduce_scatter | solution.py:245
  576.2 9.6 all-to-all-start.6
  604.6 18.1 %all-to-all-start.7 = ((bf16[512,3,1,192]{3,1,2,0:T(4,128)(2,1)}), bf16[512,3,1,192]{3,1,2,0:T(4,128)(2,1)S(1)}, u32[]{:S(2)}, u32[]{:S(2)}) async-start(bf16[512,3,1,192]{3,1,2,0:T(4,128)(2,1)} %pad_maximum_fusion.5), calls=%async_computation.7 | async-start | bytes 2097152 | tf_op jit(solution)/shard_map/all_to_all | solution.py:226
  608.2 601.2 %reduce-scatter.5.cloned.1.call-start = ((), (), s32[]{:S(2)}) async-start(), calls=%async_computation.12 | async-start | bytes 19021824 | tf_op jit(solution)/shard_map/reduce_scatter | solution.py:245
  639.2 631.9 %all-reduce.7.cloned.1.call-start = ((), (), s32[]{:S(2)}) async-start(), calls=%async_computation.24 | async-start | bytes 5111808 | tf_op jit(solution)/shard_map/psum | solution.py:266
  922.3 289.9 %copy-start.37 = (bf16[128,1152]{1,0:T(8,128)(2,1)S(1)}, bf16[128,1152]{1,0:T(8,128)(2,1)}, u32[]{:S(2)}) copy-start(bf16[128,1152]{1,0:T(8,128)(2,1)} %copy-done.36) | copy-start | bytes 884740
  922.3 289.9 %copy-start.43 = (bf16[1,1152,768]{2,1,0:T(8,128)(2,1)S(1)}, bf16[1,1152,768]{2,1,0:T(8,128)(2,1)}, u32[]{:S(2)}) copy-start(bf16[1,1152,768]{2,1,0:T(8,128)(2,1)} %all-gather.33.cloned.1.call-done) | copy-start | bytes 5308420
  (88 other events, 273.7 us)
Sparse Core Ops, SparseCore 0:
  10.8 70.4 all-gather.18
  84.1 41.6 all-gather.20
  128.5 64.6 all-gather.22
  195.2 44.4 all-gather.24
  242.3 64.1 all-gather.26
  308.5 39.5 all-gather.28
  350.3 63.9 all-gather.30
  416.5 44.4 all-gather.32
  469.6 78.0 reduce-scatter.10
  551.1 78.4 reduce-scatter.8
  633.5 286.0 reduce-scatter.6
  923.8 285.5 reduce-scatter.4
  1212.6 58.4 all-reduce.6
where the time goes:
time: 1300 us; the launch traced here: 1290 us
  waiting for transfers between devices  930 us (72%)
  blocking collectives  95.3 us (7%)
  matrix products  92 us (7%)
  local copies, waits for them, and re-layouts  68.6 us (5%)
  other arithmetic  63.5 us (5%)
  starting transfers between devices  23.9 us (2%)
  between operations  15.8 us (1%)
    reduce_scatter x2, waiting for transfers between devices, on_device(): lax.psum_scatter(jnp.concatenate([jnp.dot(normed.T, grad_qkv, preferred_e...  564 us
    all_gather x2, waiting for transfers between devices, on_device(): lax.all_gather(w_in[layer_at], 'fsdp', axis=0, tiled=True)  108 us
    all_gather x2, waiting for transfers between devices, on_device(): lax.all_gather(w_qkv[layer_at], 'fsdp', axis=0, tiled=True)  87.7 us
    all_gather x2, waiting for transfers between devices, on_device(): lax.all_gather(w_ff_out[layer_at], 'fsdp', axis=0, tiled=True)  83.5 us
    all_gather x2, blocking collectives, on_device(): lax.all_gather(gains[layer_at], 'fsdp', axis=1, tiled=True)  65.4 us
    psum x1, waiting for transfers between devices, on_device(): lax.psum(model_share.astype(jnp.bfloat16), 'seq').astype(jnp.float32)  56.8 us
  transfers between devices with their start and end apart: 19, of which 13 were waited for; matrix products, arithmetic and copies ran while one was open for 14% of the time, Pallas kernels for 0%

commit v1 on v0

v1 whole, which is shorter than its diff:
```python
import functools

import jax
import jax.numpy as jnp
from jax import lax
from jax.experimental import pallas as pl
from jax.experimental.pallas import tpu as pltpu
from jax.sharding import PartitionSpec as P

D = 768
HEADS = 12
HEAD = 64
FF = 1152
LAYERS = 2
HALF_WINDOW = 64


EPS = 1e-05
NEG = -1e30
LOCAL_BASE = 10000.0
GLOBAL_BASE = 160000.0


def layer_norm(stream, gain):
    mean_row = jnp.mean(stream, axis=-1, keepdims=True)
    centred = stream - mean_row
    spread = jnp.mean(centred * centred, axis=-1, keepdims=True)
    return centred * lax.rsqrt(spread + EPS) * gain


def geglu(lifted):
    half_width = lifted.shape[-1] // 2
    return jax.nn.gelu(lifted[:, :half_width], approximate=False) * lifted[:, half_width:]


def doc_layout(cu_row, group_rows):
    places = jnp.arange(group_rows, dtype=jnp.int32)
    inner_cuts = cu_row[1:-1]
    doc_ids = jnp.sum((places[:, None] >= inner_cuts[None, :]).astype(jnp.int32), axis=1)
    heads_of = cu_row[:-1]
    starts = jnp.max(jnp.where(places[:, None] >= heads_of[None, :], heads_of[None, :], 0), axis=1)
    return (doc_ids, places - starts)


def rope_tables(positions, base_freq):
    freqs = base_freq ** (-jnp.arange(0, HEAD, 2, dtype=jnp.float32) / HEAD)
    angles = positions.astype(jnp.float32)[:, None] * freqs[None, :]
    angles = jnp.concatenate([angles, angles], axis=1)
    return (jnp.cos(angles), jnp.sin(angles))


def meet_peers(me, count):
    barrier = pltpu.get_barrier_semaphore()
    for step in range(1, count):
        pl.semaphore_signal(
            barrier,
            inc=1,
            device_id={"seq": lax.rem(me + step, count)},
            device_id_type=pl.DeviceIdType.MESH,
        )
    pl.semaphore_wait(barrier, count - 1)


def swap_body(count, same, add, own_ref, out_ref, *scratch):
    if add:
        land_ref, send_sem, recv_sem = scratch
    else:
        send_sem, recv_sem = scratch
        land_ref = out_ref
    me = lax.axis_index("seq")
    meet_peers(me, count)
    copies = []
    for step in range(1, count):
        peer = lax.rem(me + step, count)
        copy = pltpu.make_async_remote_copy(
            src_ref=own_ref if same else own_ref.at[peer],
            dst_ref=land_ref.at[me],
            send_sem=send_sem.at[step - 1],
            recv_sem=recv_sem.at[step - 1],
            device_id={"seq": peer},
            device_id_type=pl.DeviceIdType.MESH,
        )
        copy.start()
        copies.append(copy)
    land_ref[me] = own_ref[...] if same else own_ref[me]
    for copy in copies:
        copy.wait()
    if add:
        total = land_ref[0].astype(jnp.float32)
        for at in range(1, count):
            total = total + land_ref[at].astype(jnp.float32)
        out_ref[...] = total


def swap(blocks, call_id, same=False, add=False):
    count = lax.axis_size("seq")
    piece = blocks.shape if same else blocks.shape[1:]
    out = jax.ShapeDtypeStruct(piece, jnp.float32)
    land = [pltpu.VMEM((count,) + piece, blocks.dtype)]
    if not add:
        out = jax.ShapeDtypeStruct((count,) + piece, blocks.dtype)
        land = []
    return pl.pallas_call(
        functools.partial(swap_body, count, same, add),
        out_shape=out,
        in_specs=[pl.BlockSpec(memory_space=pltpu.VMEM)],
        out_specs=pl.BlockSpec(memory_space=pltpu.VMEM),
        scratch_shapes=land
        + [pltpu.SemaphoreType.DMA((count - 1,)), pltpu.SemaphoreType.DMA((count - 1,))],
        compiler_params=pltpu.CompilerParams(
            collective_id=call_id, has_side_effects=True, vmem_limit_bytes=16 * 2**20
        ),
    )(blocks)


def gather_group(rows):
    return swap(rows, 0, same=True).reshape(-1, rows.shape[1])


def scatter_group(partial):
    count = lax.axis_size("seq")
    rows = partial.astype(jnp.bfloat16).reshape(count, -1, partial.shape[1])
    return swap(rows, 1, add=True)


def dot(left, right):
    return jnp.dot(left, right, preferred_element_type=jnp.float32)


def dot_t(left, right):
    return lax.dot_general(left, right, (((1,), (1,)), ((), ())), preferred_element_type=jnp.float32)


def t_dot(left, right):
    return lax.dot_general(left, right, (((0,), (0,)), ((), ())), preferred_element_type=jnp.float32)


def turn(values, cosine, sine_tab):
    half_width = HEAD // 2
    turned = jnp.concatenate([-values[..., half_width:], values[..., :half_width]], axis=-1)
    return values * cosine + turned * sine_tab


def turn_back(gradient, cosine, sine_tab):
    half_width = HEAD // 2
    scaled = gradient * sine_tab
    turned = jnp.concatenate([scaled[..., half_width:], -scaled[..., :half_width]], axis=-1)
    return gradient * cosine + turned


def on_device(hidden_in, cu_lengths, w_qkv, w_attn_out, w_in, w_ff_out, gains, cotangent):
    local_rows = hidden_in.shape[0]
    seq_count = lax.axis_size("seq")
    seq_at = lax.axis_index("seq")
    shards = lax.axis_size("fsdp")
    group_rows = local_rows * seq_count
    part_width = D // seq_count
    part_heads = part_width // HEAD
    part_ff = FF // seq_count
    ff_rows = w_ff_out.shape[1]
    spread_ff = ff_rows % seq_count == 0
    scale = HEAD**-0.5

    doc_ids, positions = doc_layout(cu_lengths[0], group_rows)
    places = jnp.arange(group_rows, dtype=jnp.int32)
    same_doc = doc_ids[:, None] == doc_ids[None, :]
    distance = jnp.abs(places[:, None] - places[None, :])

    def own_columns(weight):
        cut = weight.reshape(LAYERS, weight.shape[1], 3, seq_count, part_width)
        return lax.dynamic_index_in_dim(cut, seq_at, 3, keepdims=False).reshape(
            LAYERS, weight.shape[1], 3 * part_width
        )

    qkv_cut = own_columns(w_qkv)
    if spread_ff:
        unit = ff_rows // seq_count
        cut = w_in.reshape(LAYERS, w_in.shape[1], 2, shards, seq_count, unit)
        lift_cut = lax.dynamic_index_in_dim(cut, seq_at, 4, keepdims=False)
        down_cut = lax.dynamic_slice_in_dim(w_ff_out, seq_at * unit, unit, 1)
    else:
        cut = w_in.reshape(LAYERS, w_in.shape[1], 2, seq_count, part_ff)
        lift_cut = lax.dynamic_index_in_dim(cut, seq_at, 3, keepdims=False)
        down_cut = w_ff_out
    lift_cut = lift_cut.reshape(LAYERS, w_in.shape[1], 2 * part_ff)
    gain_cut = gains.reshape(LAYERS * 2, -1).T

    def collect(shard):
        return lax.all_gather(shard, "fsdp", axis=0, tiled=True)

    weights = []
    for layer_at in range(LAYERS):
        first = [qkv_cut[layer_at]]
        if layer_at == 0:
            first.append(gain_cut)
        rest = jnp.concatenate([w_attn_out[layer_at], lift_cut[layer_at]], axis=1)
        first = collect(jnp.concatenate(first, axis=1))
        rest = collect(rest)
        down = collect(down_cut[layer_at])
        if not spread_ff:
            down = lax.dynamic_slice_in_dim(down, seq_at * part_ff, part_ff, 0)
        if layer_at == 0:
            gain_full = first[:, 3 * part_width :].T.astype(jnp.float32)
        weights.append((first[:, : 3 * part_width], rest[:, :D], rest[:, D:], down))
    gain_full = gain_full.reshape(LAYERS, 2, 1, D)

    stream = hidden_in.astype(jnp.float32)
    stored = []
    for layer_at in range(LAYERS):
        qkv_w, proj_w, lift_w, down_w = weights[layer_at]
        reach = HALF_WINDOW if layer_at == 0 else group_rows
        base_freq = LOCAL_BASE if layer_at == 0 else GLOBAL_BASE
        cosine, sine_tab = rope_tables(positions, base_freq)
        allowed = same_doc & (distance <= reach)
        entering = stream
        normed = layer_norm(stream, gain_full[layer_at, 0]).astype(jnp.bfloat16)
        normed_all = gather_group(normed)
        qkv = dot(normed_all, qkv_w)
        qkv = qkv.reshape(group_rows, 3, part_heads, HEAD).transpose(1, 2, 0, 3)
        q = turn(qkv[0], cosine, sine_tab).astype(jnp.bfloat16)
        k = turn(qkv[1], cosine, sine_tab).astype(jnp.bfloat16)
        v = qkv[2].astype(jnp.bfloat16)
        scores = jnp.einsum("hqd,hkd->hqk", q, k, preferred_element_type=jnp.float32) * scale
        scores = jnp.where(allowed[None], scores, NEG)
        expd = jnp.exp(scores - jnp.max(scores, axis=-1, keepdims=True))
        probs = expd / jnp.sum(expd, axis=-1, keepdims=True)
        mixture = jnp.einsum(
            "hqk,hkd->qhd", probs.astype(jnp.bfloat16), v, preferred_element_type=jnp.float32
        )
        mixture = mixture.astype(jnp.bfloat16).reshape(group_rows, part_width)
        mix_all = swap(mixture, 2, same=True)
        returned = lax.dynamic_slice_in_dim(mix_all, seq_at * local_rows, local_rows, 1)
        returned = returned.transpose(1, 0, 2).reshape(local_rows, D)
        stream = stream + dot(returned, proj_w)
        middle = stream
        normed_ff = layer_norm(stream, gain_full[layer_at, 1]).astype(jnp.bfloat16)
        normed_ff_all = gather_group(normed_ff)
        lifted = dot(normed_ff_all, lift_w)
        gated = geglu(lifted).astype(jnp.bfloat16)
        stream = stream + scatter_group(dot(gated, down_w))
        stored.append(
            (
                entering,
                normed_all,
                q,
                k,
                v,
                probs,
                allowed,
                cosine,
                sine_tab,
                mix_all,
                middle,
                normed_ff_all,
                lifted,
                gated,
            )
        )
    block_out = stream.astype(jnp.bfloat16)
    gradient = cotangent.astype(jnp.float32)
    grads = [None] * LAYERS
    for layer_at in reversed(range(LAYERS)):
        (
            entering,
            normed_all,
            q,
            k,
            v,
            probs,
            allowed,
            cosine,
            sine_tab,
            mix_all,
            middle,
            normed_ff_all,
            lifted,
            gated,
        ) = stored[layer_at]
        qkv_w, proj_w, lift_w, down_w = weights[layer_at]
        grad_y = gather_group(gradient.astype(jnp.bfloat16))
        _, pullback = jax.vjp(geglu, lifted)
        grad_lift = pullback(dot_t(grad_y, down_w))[0].astype(jnp.bfloat16)
        grad_normed = scatter_group(dot_t(grad_lift, lift_w))
        _, pullback = jax.vjp(layer_norm, middle, gain_full[layer_at, 1])
        grad_input, gain_ffn = pullback(grad_normed)
        gradient = gradient + grad_input
        grad_a = gradient.astype(jnp.bfloat16)
        grad_mix = dot_t(grad_a, proj_w).astype(jnp.bfloat16)
        pair = jnp.stack(
            [
                grad_mix.reshape(local_rows, seq_count, part_width),
                grad_a.reshape(local_rows, seq_count, part_width),
            ]
        ).transpose(2, 0, 1, 3)
        pair = swap(pair, 3)
        grad_heads = (
            pair[:, 0].reshape(group_rows, part_heads, HEAD).transpose(1, 0, 2)
        )
        grad_a_part = pair[:, 1].reshape(group_rows, part_width)
        grad_probs = jnp.einsum("hqd,hkd->hqk", grad_heads, v, preferred_element_type=jnp.float32)
        centre = jnp.sum(probs * grad_probs, axis=-1, keepdims=True)
        grad_scores = (probs * (grad_probs - centre)).astype(jnp.bfloat16)
        grad_q = jnp.einsum("hqk,hkd->hqd", grad_scores, k, preferred_element_type=jnp.float32)
        grad_k = jnp.einsum("hqk,hqd->hkd", grad_scores, q, preferred_element_type=jnp.float32)
        grad_v = jnp.einsum(
            "hqk,hqd->hkd",
            probs.astype(jnp.bfloat16),
            grad_heads,
            preferred_element_type=jnp.float32,
        )
        grad_qkv = jnp.stack(
            [
                turn_back(grad_q * scale, cosine, sine_tab),
                turn_back(grad_k * scale, cosine, sine_tab),
                grad_v,
            ]
        ).astype(jnp.bfloat16)
        grad_qkv = grad_qkv.transpose(2, 0, 1, 3).reshape(group_rows, 3 * part_width)
        grad_normed = scatter_group(dot_t(grad_qkv, qkv_w))
        _, pullback = jax.vjp(layer_norm, entering, gain_full[layer_at, 0])
        grad_input, gain_attn = pullback(grad_normed)
        gradient = gradient + grad_input

        proj_grad = lax.dot_general(
            mix_all,
            grad_a_part,
            (((1,), (0,)), ((), ())),
            preferred_element_type=jnp.float32,
        ).reshape(D, part_width)
        early = jnp.concatenate(
            [t_dot(normed_ff_all, grad_lift), proj_grad], axis=1
        ).astype(jnp.bfloat16)
        late = jnp.concatenate(
            [t_dot(normed_all, grad_qkv), gain_attn.T, gain_ffn.T], axis=1
        ).astype(jnp.bfloat16)
        down_grad = t_dot(gated, grad_y).astype(jnp.bfloat16)
        if not spread_ff:
            wide = jnp.zeros((FF, D), jnp.bfloat16)
            down_grad = lax.dynamic_update_slice_in_dim(wide, down_grad, seq_at * part_ff, 0)
        sums = [
            lax.psum_scatter(part, "fsdp", scatter_dimension=0, tiled=True)
            for part in (down_grad, early, late)
        ]
        grads[layer_at] = [
            lax.all_gather(part, "seq", axis=0, tiled=False).astype(jnp.float32) for part in sums
        ]

    def whole(parts, blocks, width):
        parts = parts.reshape(seq_count, -1, blocks, width)
        return parts.transpose(1, 2, 0, 3).reshape(parts.shape[1], blocks * seq_count * width)

    out = [[], [], [], [], []]
    for down, early, late in grads:
        out[0].append(whole(late[:, :, : 3 * part_width], 3, part_width))
        out[1].append(whole(early[:, :, 2 * part_ff :], 1, part_width))
        lift = early[:, :, : 2 * part_ff]
        if spread_ff:
            out[2].append(whole(lift, 2 * shards, ff_rows // seq_count))
            out[3].append(down.reshape(ff_rows, D))
        else:
            out[2].append(whole(lift, 2, part_ff))
            out[3].append(jnp.sum(down, axis=0))
        out[4].append(jnp.sum(late[:, :, 3 * part_width :], axis=0).T)
    return (block_out, gradient, *[jnp.stack(member) for member in out])


def solution(mesh):
    return jax.shard_map(
        on_device,
        mesh=mesh,
        in_specs=(
            P(("fsdp", "seq"), None),
            P("fsdp", None),
            P(None, "fsdp", None),
            P(None, "fsdp", None),
            P(None, "fsdp", None),
            P(None, "fsdp", None),
            P(None, None, "fsdp"),
            P(("fsdp", "seq"), None),
        ),
        out_specs=(
            P(("fsdp", "seq"), None),
            P(("fsdp", "seq"), None),
            P(None, "fsdp", None),
            P(None, "fsdp", None),
            P(None, "fsdp", None),
            P(None, "fsdp", None),
            P(None, None, "fsdp"),
        ),
        check_vma=False,
    )
```

time: 1300 us -> 676 us (0.52)
  waiting for transfers between devices: 930 us -> 95.7 us
  Pallas kernels: 0 us -> 174 us
  blocking collectives: 95.3 us -> 215 us
  matrix products: 92 us -> 55.6 us
  other arithmetic: 63.5 us -> 36.4 us
  starting transfers between devices: 23.9 us -> 5.06 us
    reduce_scatter x4, waiting for transfers between devices: 564 us -> 94.8 us  [on_device(): lax.psum_scatter(part, 'fsdp', scatter_dimension=0, tiled=True)]
    all_gather x8 -> x2, waiting for transfers between devices: 291 us -> 0.04 us  [collect(): return lax.all_gather(shard, 'fsdp', axis=0, tiled=True)]
    pallas_call x0 -> x16, Pallas kernels: none -> 174 us  [swap(): pl.pallas_call(functools.partial(swap_body, count, same, add), out_shape=...]
    all_gather x2 -> x10, blocking collectives: 65.4 us -> 183 us  [the longest x4 142 us: collect(): return lax.all_gather(shard, 'fsdp', axis=0, tiled=True)]
    psum x1 -> x0, waiting for transfers between devices: 56.8 us -> none  [on_device(): lax.psum(model_share.astype(jnp.bfloat16), 'seq').astype(jnp.float32)]
    dot_general x36 -> x34, matrix products: 92 us -> 48.6 us  [the longest x8 13.7 us: dot_t(): lax.dot_general(left, right, (((1,), (1,)), ((), ())), preferred_element_...]
    unnamed x0 -> x1, blocking collectives: none -> 32.5 us
    all_to_all x2 -> x0, blocking collectives: 29.9 us -> none  [the longest x1 17.8 us: on_device(): lax.all_to_all(grad_stack, 'seq', split_axis=0, concat_axis=2, tiled=True)]
  transfers between devices with their start and end apart: 19 -> 8, of which waited for: 13 -> 3; matrix products, arithmetic and copies ran while one was open for 14% -> 19% of each run, Pallas kernels for 0% -> 18%
where the time goes in v1:
time: 676 us; the launch traced here: 668 us
  blocking collectives  215 us (32%)
  Pallas kernels  174 us (26%)
  waiting for transfers between devices  95.7 us (14%)
  local copies, waits for them, and re-layouts  69.1 us (10%)
  matrix products  55.6 us (8%)
  other arithmetic  36.4 us (5%)
  between operations  17.1 us (3%)
    pallas_call x16, Pallas kernels, swap(): pl.pallas_call(functools.partial(swap_body, count, same, add), out_shape=...  174 us
    all_gather x4, blocking collectives, collect(): return lax.all_gather(shard, 'fsdp', axis=0, tiled=True)  142 us
    reduce_scatter x4, waiting for transfers between devices, on_device(): lax.psum_scatter(part, 'fsdp', scatter_dimension=0, tiled=True)  94.8 us
    all_gather x6, blocking collectives, on_device(): lax.all_gather(part, 'seq', axis=0, tiled=False).astype(jnp.float32)  41.4 us
    unnamed x1, blocking collectives  32.5 us
    unnamed x189, local copies, waits for them, and re-layouts  21.2 us
    dot_general x8, matrix products, dot_t(): lax.dot_general(left, right, (((1,), (1,)), ((), ())), preferred_element_...  13.7 us
  transfers between devices with their start and end apart: 8, of which 3 were waited for; matrix products, arithmetic and copies ran while one was open for 19% of the time, Pallas kernels for 18%

profile of v1, /device:TPU:0, one launch (start us, length us, event | category | flops | bytes accessed | tf_op | source)
XLA Modules:
  0.0 668.0 jit_solution(7254171932388568919)
XLA Ops:
  8.2 3.1 copy.317
  17.4 36.2 %all_gather.54 = bf16[768,580]{1,0:T(8,128)(2,1)S(1)} all-gather(bf16[96,580]{1,0:T(8,128)(2,1)S(1)} %copy.311), channel_id=1, replica_groups=mesh['fsdp'=8,'seq'=4] {'fsdp'}, dimensions={0}, use_global_device_ids=true | all-gather | bytes 1002240 | tf_op jit(solution)/shard_map/all_gather | solution.py:189
  58.3 35.5 %all-gather = bf16[1,288,768]{2,0,1:T(2,128)(2,1)} all-gather(bf16[1,36,768]{2,0,1:T(2,128)(2,1)S(1)} %copy.384), channel_id=2, replica_groups=mesh['fsdp'=8,'seq'=4] {'fsdp'}, dimensions={1}, use_global_device_ids=true | all-gather | bytes 497664 | tf_op jit(solution)/shard_map/all_gather | solution.py:189
  93.8 36.4 %all-gather.1 = bf16[1,288,768]{2,0,1:T(2,128)(2,1)} all-gather(bf16[1,36,768]{2,0,1:T(2,128)(2,1)S(1)} %copy.385), channel_id=3, replica_groups=mesh['fsdp'=8,'seq'=4] {'fsdp'}, dimensions={1}, use_global_device_ids=true | all-gather | bytes 497664 | tf_op jit(solution)/shard_map/all_gather | solution.py:189
  130.2 10.2 %shard_map.143 = bf16[4,128,768]{2,1,0:T(8,128)(2,1)S(1)} custom-call(bf16[128,768]{1,0:T(8,128)(2,1)S(1)} %copy-done.9), custom_call_target="tpu_custom_call" | custom-call | tf_op jit(solution)/shard_map/pallas_call | solution.py:103
  141.1 10.9 %shard_map.135 = bf16[4,128,768]{2,1,0:T(8,128)(2,1)S(1)} custom-call(bf16[128,768]{1,0:T(8,128)(2,1)S(1)} %fusion.56.own_ref), custom_call_target="tpu_custom_call" | custom-call | tf_op jit(solution)/shard_map/pallas_call | solution.py:103
  152.1 33.4 %all_gather.57 = bf16[768,576]{1,0:T(8,128)(2,1)S(1)} all-gather(bf16[96,576]{1,0:T(8,128)(2,1)S(1)} %copy.320), channel_id=1, replica_groups=mesh['fsdp'=8,'seq'=4] {'fsdp'}, dimensions={0}, use_global_device_ids=true | all-gather | bytes 995328 | tf_op jit(solution)/shard_map/all_gather | solution.py:189
  194.1 3.0 fusion.132
  199.7 12.3 %shard_map.136 = bf16[4,512,192]{2,1,0:T(8,128)(2,1)S(1)} custom-call(bf16[512,192]{1,0:T(8,128)(2,1)S(1)} %copy.315.own_ref), custom_call_target="tpu_custom_call" | custom-call | tf_op jit(solution)/shard_map/pallas_call | solution.py:103
  214.8 10.9 %shard_map.137 = bf16[4,128,768]{2,1,0:T(8,128)(2,1)S(1)} custom-call(bf16[128,768]{1,0:T(8,128)(2,1)S(1)} %multiply_convert_fusion.6.own_ref), custom_call_target="tpu_custom_call" | custom-call | tf_op jit(solution)/shard_map/pallas_call | solution.py:103
  230.7 11.0 %shard_map.138 = f32[128,768]{1,0:T(8,128)S(1)} custom-call(bf16[4,128,768]{2,1,0:T(8,128)(2,1)S(1)} %bitcast.275), custom_call_target="tpu_custom_call" | custom-call | tf_op jit(solution)/shard_map/pallas_call | solution.py:103
  242.8 10.9 %shard_map.139 = bf16[4,128,768]{2,1,0:T(8,128)(2,1)S(1)} custom-call(bf16[128,768]{1,0:T(8,128)(2,1)S(1)} %multiply_convert_fusion.5.own_ref), custom_call_target="tpu_custom_call" | custom-call | tf_op jit(solution)/shard_map/pallas_call | solution.py:103
  255.5 4.0 fusion.134
  262.1 13.7 %shard_map.140 = bf16[4,512,192]{2,1,0:T(8,128)(2,1)S(1)} custom-call(bf16[512,192]{1,0:T(8,128)(2,1)S(1)} %copy.323.own_ref), custom_call_target="tpu_custom_call" | custom-call | tf_op jit(solution)/shard_map/pallas_call | solution.py:103
  278.4 10.9 %shard_map.141 = bf16[4,128,768]{2,1,0:T(8,128)(2,1)S(1)} custom-call(bf16[128,768]{1,0:T(8,128)(2,1)S(1)} %multiply_convert_fusion.4.own_ref), custom_call_target="tpu_custom_call" | custom-call | tf_op jit(solution)/shard_map/pallas_call | solution.py:103
  292.6 11.0 %shard_map.142 = f32[128,768]{1,0:T(8,128)S(1)} custom-call(bf16[4,128,768]{2,1,0:T(8,128)(2,1)S(1)} %bitcast.273), custom_call_target="tpu_custom_call" | custom-call | tf_op jit(solution)/shard_map/pallas_call | solution.py:103
  304.7 11.0 %shard_map.144 = f32[128,768]{1,0:T(8,128)S(1)} custom-call(bf16[4,128,768]{2,1,0:T(8,128)(2,1)S(1)} %bitcast.276), custom_call_target="tpu_custom_call" | custom-call | tf_op jit(solution)/shard_map/pallas_call | solution.py:103
  328.4 8.1 %shard_map.145 = bf16[4,2,128,192]{3,2,1,0:T(8,128)(2,1)S(1)} custom-call(bf16[4,2,128,192]{3,2,1,0:T(8,128)(2,1)S(1)} %maximum_bitcast_fusion.own_ref), custom_call_target="tpu_custom_call" | custom-call | tf_op jit(solution)/shard_map/pallas_call | solution.py:103
  350.5 11.0 %shard_map.146 = f32[128,768]{1,0:T(8,128)S(1)} custom-call(bf16[4,128,768]{2,1,0:T(8,128)(2,1)S(1)} %bitcast.272), custom_call_target="tpu_custom_call" | custom-call | tf_op jit(solution)/shard_map/pallas_call | solution.py:103
  367.7 10.9 %shard_map.147 = bf16[4,128,768]{2,1,0:T(8,128)(2,1)S(1)} custom-call(bf16[128,768]{1,0:T(8,128)(2,1)S(1)} %get-tuple-element.76.own_ref), custom_call_target="tpu_custom_call" | custom-call | tf_op jit(solution)/shard_map/pallas_call | solution.py:103
  383.2 11.0 %shard_map.148 = f32[128,768]{1,0:T(8,128)S(1)} custom-call(bf16[4,128,768]{2,1,0:T(8,128)(2,1)S(1)} %bitcast.277), custom_call_target="tpu_custom_call" | custom-call | tf_op jit(solution)/shard_map/pallas_call | solution.py:103
  401.5 8.4 %shard_map.149 = bf16[4,2,128,192]{3,2,1,0:T(8,128)(2,1)S(1)} custom-call(bf16[4,2,128,192]{3,2,1,0:T(8,128)(2,1)S(1)} %maximum_bitcast_fusion.1.own_ref), custom_call_target="tpu_custom_call" | custom-call | tf_op jit(solution)/shard_map/pallas_call | solution.py:103
  419.0 11.0 %shard_map.150 = f32[128,768]{1,0:T(8,128)S(1)} custom-call(bf16[4,128,768]{2,1,0:T(8,128)(2,1)S(1)} %bitcast.274), custom_call_target="tpu_custom_call" | custom-call | tf_op jit(solution)/shard_map/pallas_call | solution.py:103
  451.1 32.5 %fusion.118 = (bf16[40,768]{1,0:T(8,128)(2,1)S(1)}, bf16[40,768]{1,0:T(8,128)(2,1)S(1)}) fusion(bf16[288,768]{1,0:T(8,128)(2,1)S(1)} %convolution_convert_fusion.10, bf16[288,768]{1,0:T(8,128)(2,1)S(1)} %convolution_convert_fusion.11), kind=kCustom, calls=%all-reduce-scatter.2 | all-reduce-scatter fusion | flops 491521 | bytes 1008128
  490.2 5.7 all-gather.9
  496.2 5.8 all-gather.8
  503.0 7.3 %all-gather.3 = bf16[384,578]{1,0:T(8,128)(2,1)S(1)} all-gather(bf16[96,578]{1,0:T(8,128)(2,1)} %reduce-scatter.19.cloned.1.call-done), channel_id=5, replica_groups=mesh['fsdp'=8,'seq'=4] {'seq'}, dimensions={0}, use_global_device_ids=true | all-gather | bytes 554880 | tf_op jit(solution)/shard_map/all_gather | solution.py:345
  511.4 7.3 %all-gather.2 = bf16[384,578]{1,0:T(8,128)(2,1)S(1)} all-gather(bf16[96,578]{1,0:T(8,128)(2,1)} %reduce-scatter.17.cloned.1.call-done), channel_id=4, replica_groups=mesh['fsdp'=8,'seq'=4] {'seq'}, dimensions={0}, use_global_device_ids=true | all-gather | bytes 554880 | tf_op jit(solution)/shard_map/all_gather | solution.py:345
  533.1 38.3 %reduce-scatter.23.cloned.1.call-done = bf16[96,768]{1,0:T(8,128)(2,1)} async-done(((bf16[768,768]{1,0:T(8,128)(2,1)}), bf16[96,768]{1,0:T(8,128)(2,1)}) %reduce-scatter.23.cloned.1.call-update) | async-done | bytes 147472 | tf_op jit(solution)/shard_map/reduce_scatter | solution.py:341
  571.4 7.7 %all-gather.5 = bf16[384,768]{1,0:T(8,128)(2,1)S(1)} all-gather(bf16[96,768]{1,0:T(8,128)(2,1)} %reduce-scatter.23.cloned.1.call-done), channel_id=7, replica_groups=mesh['fsdp'=8,'seq'=4] {'seq'}, dimensions={0}, use_global_device_ids=true | all-gather | bytes 737280 | tf_op jit(solution)/shard_map/all_gather | solution.py:345
  581.2 56.5 %reduce-scatter.21.cloned.1.call-done = bf16[96,768]{1,0:T(8,128)(2,1)} async-done(((bf16[768,768]{1,0:T(8,128)(2,1)}), bf16[96,768]{1,0:T(8,128)(2,1)}) %reduce-scatter.21.cloned.1.call-update) | async-done | bytes 147472 | tf_op jit(solution)/shard_map/reduce_scatter | solution.py:341
  637.7 7.6 %all-gather.4 = bf16[384,768]{1,0:T(8,128)(2,1)S(1)} all-gather(bf16[96,768]{1,0:T(8,128)(2,1)} %reduce-scatter.21.cloned.1.call-done), channel_id=6, replica_groups=mesh['fsdp'=8,'seq'=4] {'seq'}, dimensions={0}, use_global_device_ids=true | all-gather | bytes 737280 | tf_op jit(solution)/shard_map/all_gather | solution.py:345
  (399 shorter events, 157.0 us)
Async XLA Ops:
  7.2 205.1 %all-gather.13.cloned.1.call-start = ((), (), s32[]{:S(2)}) async-start(), calls=%async_computation.4 | async-start | bytes 2433024 | tf_op jit(solution)/shard_map/all_gather | solution.py:189
  14.0 262.0 %all-gather.15.cloned.1.call-start = ((), (), s32[]{:S(2)}) async-start(), calls=%async_computation.5 | async-start | bytes 2433024 | tf_op jit(solution)/shard_map/all_gather | solution.py:189
  15.1 487.9 %reduce-scatter.19.cloned.1.call-start = ((), (), s32[]{:S(2)}) async-start(), calls=%async_computation.7 | async-start | bytes 1105920 | tf_op jit(solution)/shard_map/reduce_scatter | solution.py:341
  17.4 37.5 %copy-start.14 = (bf16[128,768]{1,0:T(8,128)(2,1)S(1)}, bf16[128,768]{1,0:T(8,128)(2,1)}, u32[]{:S(2)}) copy-start(bf16[128,768]{1,0:T(8,128)(2,1)} %param.8) | copy-start | bytes 589828
  54.9 75.3 %copy-start.9 = (bf16[128,768]{1,0:T(8,128)(2,1)S(1)}, bf16[128,768]{1,0:T(8,128)(2,1)}, u32[]{:S(2)}) copy-start(bf16[128,768]{1,0:T(8,128)(2,1)} %own_ref) | copy-start | bytes 589828
  55.0 85.9 %copy-start.57 = (f32[128]{0:T(128)}, f32[128]{0:T(128)S(1)}, u32[]{:S(2)}) copy-start(f32[128]{0:T(128)S(1)} %broadcast_multiply_fusion.13) | copy-start | bytes 1540
  55.2 85.7 %copy-start.67 = (f32[128]{0:T(128)}, f32[128]{0:T(128)S(1)}, u32[]{:S(2)}) copy-start(f32[128]{0:T(128)S(1)} %fusion.105) | copy-start | bytes 1540
  152.1 36.9 %copy-start.2 = (bf16[4,128,768]{2,1,0:T(8,128)(2,1)}, bf16[4,128,768]{2,1,0:T(8,128)(2,1)S(1)}, u32[]{:S(2)}) copy-start(bf16[4,128,768]{2,1,0:T(8,128)(2,1)S(1)} %shard_map.135) | copy-start | bytes 2359300
  213.9 27.8 %copy-start.12 = (f32[128,768]{1,0:T(8,128)}, f32[128,768]{1,0:T(8,128)S(1)}, u32[]{:S(2)}) copy-start(f32[128,768]{1,0:T(8,128)S(1)} %get-tuple-element.150) | copy-start | bytes 1179652
  241.9 12.5 %copy-start.61 = (f32[128]{0:T(128)}, f32[128]{0:T(128)S(1)}, u32[]{:S(2)}) copy-start(f32[128]{0:T(128)S(1)} %broadcast_multiply_fusion.11) | copy-start | bytes 1540
  242.1 12.3 %copy-start.78 = (f32[128]{0:T(128)}, f32[128]{0:T(128)S(1)}, u32[]{:S(2)}) copy-start(f32[128]{0:T(128)S(1)} %multiply_reduce_fusion.9) | copy-start | bytes 1540
  242.1 12.3 %copy-start.71 = (f32[128]{0:T(128)}, f32[128]{0:T(128)S(1)}, u32[]{:S(2)}) copy-start(f32[128]{0:T(128)S(1)} %fusion.107) | copy-start | bytes 1540
  276.0 13.3 %copy-start.34 = (bf16[768,1344]{1,0:T(8,128)(2,1)S(1)}, bf16[768,1344]{1,0:T(8,128)(2,1)}, u32[]{:S(2)}) copy-start(bf16[768,1344]{1,0:T(8,128)(2,1)} %all-gather.15.cloned.1.call-done) | copy-start | bytes 6193156
  291.9 12.8 %copy-start.50 = (f32[512,288]{0,1:T(8,128)}, f32[512,288]{0,1:T(8,128)S(1)}, u32[]{:S(2)}) copy-start(f32[512,288]{0,1:T(8,128)S(1)} %get-tuple-element.90) | copy-start | bytes 1769476
  327.3 13.6 %copy-start.66 = (f32[3,512]{1,0:T(4,128)S(1)}, f32[3,512]{1,0:T(4,128)}, u32[]{:S(2)}) copy-start(f32[3,512]{1,0:T(4,128)} %copy-done.65) | copy-start | bytes 18436
  366.1 145.3 %reduce-scatter.17.cloned.1.call-start = ((), (), s32[]{:S(2)}) async-start(), calls=%async_computation.6 | async-start | bytes 1105920 | tf_op jit(solution)/shard_map/reduce_scatter | solution.py:341
  366.4 12.3 %copy-start.22 = (f32[512,576]{0,1:T(8,128)S(1)}, f32[512,576]{0,1:T(8,128)}, u32[]{:S(2)}) copy-start(f32[512,576]{0,1:T(8,128)} %copy-done.21) | copy-start | bytes 3538948
  366.4 12.3 %copy-start.40 = (bf16[1,288,768]{2,0,1:T(2,128)(2,1)S(1)}, bf16[1,288,768]{2,0,1:T(2,128)(2,1)}, u32[]{:S(2)}) copy-start(bf16[1,288,768]{2,0,1:T(2,128)(2,1)} %all-gather) | copy-start | bytes 1327108
  367.7 27.1 %copy-start.28 = (f32[128,768]{1,0:T(8,128)}, f32[128,768]{1,0:T(8,128)S(1)}, u32[]{:S(2)}) copy-start(f32[128,768]{1,0:T(8,128)S(1)} %get-tuple-element.77) | copy-start | bytes 1179652
  380.6 13.6 %copy-start.13 = (f32[128,768]{1,0:T(8,128)S(1)}, f32[128,768]{1,0:T(8,128)}, u32[]{:S(2)}) copy-start(f32[128,768]{1,0:T(8,128)} %copy-done.12) | copy-start | bytes 1179652
  380.7 13.6 %copy-start.60 = (f32[128]{0:T(128)S(1)}, f32[128]{0:T(128)}, u32[]{:S(2)}) copy-start(f32[128]{0:T(128)} %copy-done.59) | copy-start | bytes 1540
  380.7 13.6 %copy-start.70 = (f32[128]{0:T(128)S(1)}, f32[128]{0:T(128)}, u32[]{:S(2)}) copy-start(f32[128]{0:T(128)} %copy-done.69) | copy-start | bytes 1540
  418.1 12.1 %copy-start.75 = (f32[128]{0:T(128)S(1)}, f32[128]{0:T(128)}, u32[]{:S(2)}) copy-start(f32[128]{0:T(128)} %copy-done.74) | copy-start | bytes 1540
  418.1 12.1 %copy-start.68 = (f32[128]{0:T(128)S(1)}, f32[128]{0:T(128)}, u32[]{:S(2)}) copy-start(f32[128]{0:T(128)} %copy-done.67) | copy-start | bytes 1540
  434.9 136.5 %reduce-scatter.23.cloned.1.call-start = ((), (), s32[]{:S(2)}) async-start(), calls=%async_computation.9 | async-start | bytes 1327104 | tf_op jit(solution)/shard_map/reduce_scatter | solution.py:341
  441.5 196.2 %reduce-scatter.21.cloned.1.call-start = ((), (), s32[]{:S(2)}) async-start(), calls=%async_computation.8 | async-start | bytes 1327104 | tf_op jit(solution)/shard_map/reduce_scatter | solution.py:341
  449.6 38.7 %copy-start.80 = (f32[128]{0:T(128)S(1)}, f32[128]{0:T(128)}, u32[]{:S(2)}) copy-start(f32[128]{0:T(128)} %get-tuple-element.65) | copy-start | bytes 1540
  449.6 38.7 %copy-start.16 = (bf16[128,768]{1,0:T(8,128)(2,1)S(1)}, bf16[128,768]{1,0:T(8,128)(2,1)}, u32[]{:S(2)}) copy-start(bf16[128,768]{1,0:T(8,128)(2,1)} %param.8) | copy-start | bytes 589828
  449.6 38.7 %copy-start.29 = (f32[128,768]{1,0:T(8,128)S(1)}, f32[128,768]{1,0:T(8,128)}, u32[]{:S(2)}) copy-start(f32[128,768]{1,0:T(8,128)} %copy-done.28) | copy-start | bytes 1179652
  449.6 38.7 %copy-start.31 = (f32[128,768]{1,0:T(8,128)S(1)}, f32[128,768]{1,0:T(8,128)}, u32[]{:S(2)}) copy-start(f32[128,768]{1,0:T(8,128)} %copy-done.30) | copy-start | bytes 1179652
  483.6 12.3 %collective-permute-start = (bf16[28,768]{1,0:T(8,128)(2,1)S(1)}, bf16[28,768]{1,0:T(8,128)(2,1)S(1)}, u32[]{:S(2)}, u32[]{:S(2)}) collective-permute-start(bf16[28,768]{1,0:T(8,128)(2,1)S(1)} %slice.292), channel_id=1, source_target_pairs={{0,4},{4,8},{8,12},{12,16},{16,20},{20,24},{24,28},{1,5},{5,9},{9,... | collective-permute-start | bytes 129032
  485.7 4.2 collective-permute-start.1
  (62 other events, 262.0 us)
Sparse Core Ops, SparseCore 0:
  14.2 65.9 all-gather.12
  82.3 56.2 all-gather.14
  366.2 65.0 reduce-scatter.18
  435.0 69.4 reduce-scatter.16
  508.3 63.0 reduce-scatter.22
  574.7 63.0 reduce-scatter.20

commit v2 on v1

--- a/solution.py
+++ b/solution.py
@@ -49,78 +49,210 @@
     return (jnp.cos(angles), jnp.sin(angles))
 
 
-def meet_peers(me, count):
+MESH = pl.DeviceIdType.MESH
+
+
+def meet(axis, peers):
     barrier = pltpu.get_barrier_semaphore()
-    for step in range(1, count):
-        pl.semaphore_signal(
-            barrier,
-            inc=1,
-            device_id={"seq": lax.rem(me + step, count)},
-            device_id_type=pl.DeviceIdType.MESH,
-        )
-    pl.semaphore_wait(barrier, count - 1)
-
-
-def swap_body(count, same, add, own_ref, out_ref, *scratch):
-    if add:
-        land_ref, send_sem, recv_sem = scratch
-    else:
-        send_sem, recv_sem = scratch
-        land_ref = out_ref
+    for peer in peers:
+        pl.semaphore_signal(barrier, inc=1, device_id={axis: peer}, device_id_type=MESH)
+    pl.semaphore_wait(barrier, len(peers))
+
+
+def push(axis, peer, source, target, sems, at):
+    copy = pltpu.make_async_remote_copy(
+        src_ref=source,
+        dst_ref=target,
+        send_sem=sems.at[0, at],
+        recv_sem=sems.at[1, at],
+        device_id={axis: peer},
+        device_id_type=MESH,
+    )
+    copy.start()
+    return copy
+
+
+def chip_peers():
     me = lax.axis_index("seq")
-    meet_peers(me, count)
-    copies = []
-    for step in range(1, count):
-        peer = lax.rem(me + step, count)
-        copy = pltpu.make_async_remote_copy(
-            src_ref=own_ref if same else own_ref.at[peer],
-            dst_ref=land_ref.at[me],
-            send_sem=send_sem.at[step - 1],
-            recv_sem=recv_sem.at[step - 1],
-            device_id={"seq": peer},
-            device_id_type=pl.DeviceIdType.MESH,
-        )
-        copy.start()
-        copies.append(copy)
-    land_ref[me] = own_ref[...] if same else own_ref[me]
+    chip, core = me // 2, me % 2
+    return me, 2 * chip + 1 - core, 2 * (1 - chip) + core, 2 * (1 - chip) + 1 - core
+
+
+def spread_body(own_ref, out_ref, sems):
+    me, sibling, across, _ = chip_peers()
+    meet("seq", (sibling, across))
+    far = push("seq", across, own_ref, out_ref.at[me], sems, 0)
+    near = push("seq", sibling, own_ref, out_ref.at[me], sems, 1)
+    out_ref[me] = own_ref[...]
+    far.wait_recv()
+    onward = push("seq", sibling, out_ref.at[across], out_ref.at[across], sems, 2)
+    far.wait_send()
+    near.wait()
+    onward.wait()
+
+
+def fold_body(own_ref, out_ref, land, passing, arrived, sems):
+    me, sibling, across, diagonal = chip_peers()
+    meet("seq", (sibling, across))
+    first = push("seq", sibling, own_ref.at[diagonal], land.at[0], sems, 0)
+    second = push("seq", sibling, own_ref.at[sibling], land.at[1], sems, 1)
+    first.wait_recv()
+    total = own_ref[across].astype(jnp.float32) + land[0].astype(jnp.float32)
+    passing[...] = total.astype(passing.dtype)
+    third = push("seq", across, passing, arrived, sems, 2)
+    second.wait_recv()
+    mine = own_ref[me].astype(jnp.float32) + land[1].astype(jnp.float32)
+    third.wait_recv()
+    out_ref[...] = mine + arrived[...].astype(jnp.float32)
+    first.wait_send()
+    second.wait_send()
+    third.wait_send()
+
+
+def trade_body(count, own_ref, out_ref, sems):
+    me = lax.axis_index("seq")
+    peers = [lax.rem(me + step, count) for step in range(1, count)]
+    meet("seq", peers)
+    copies = [
+        push("seq", peer, own_ref.at[peer], out_ref.at[me], sems, at)
+        for at, peer in enumerate(peers)
+    ]
+    out_ref[me] = own_ref[me]
     for copy in copies:
         copy.wait()
-    if add:
-        total = land_ref[0].astype(jnp.float32)
-        for at in range(1, count):
-            total = total + land_ref[at].astype(jnp.float32)
-        out_ref[...] = total
-
-
-def swap(blocks, call_id, same=False, add=False):
-    count = lax.axis_size("seq")
-    piece = blocks.shape if same else blocks.shape[1:]
+
+
+def call(body, out, scratch, call_id, *operands):
+    space = pl.BlockSpec(memory_space=pltpu.VMEM)
+    many = isinstance(out, list)
+    return pl.pallas_call(
+        body,
+        out_shape=out,
+        in_specs=[space] * len(operands),
+        out_specs=[space] * len(out) if many else space,
+        scratch_shapes=scratch,
+        compiler_params=pltpu.CompilerParams(
+            collective_id=call_id, has_side_effects=True, vmem_limit_bytes=40 * 2**20
+        ),
+    )(*operands)
+
+
+def pair_sems(*shape):
+    return pltpu.SemaphoreType.DMA((2,) + shape)
+
+
+def spread(rows, call_id):
+    out = jax.ShapeDtypeStruct((4,) + rows.shape, rows.dtype)
+    return call(spread_body, out, [pair_sems(3)], call_id, rows)
+
+
+def fold(blocks, call_id):
+    piece = blocks.shape[1:]
     out = jax.ShapeDtypeStruct(piece, jnp.float32)
-    land = [pltpu.VMEM((count,) + piece, blocks.dtype)]
-    if not add:
-        out = jax.ShapeDtypeStruct((count,) + piece, blocks.dtype)
-        land = []
-    return pl.pallas_call(
-        functools.partial(swap_body, count, same, add),
-        out_shape=out,
-        in_specs=[pl.BlockSpec(memory_space=pltpu.VMEM)],
-        out_specs=pl.BlockSpec(memory_space=pltpu.VMEM),
-        scratch_shapes=land
-        + [pltpu.SemaphoreType.DMA((count - 1,)), pltpu.SemaphoreType.DMA((count - 1,))],
-        compiler_params=pltpu.CompilerParams(
-            collective_id=call_id, has_side_effects=True, vmem_limit_bytes=16 * 2**20
-        ),
-    )(blocks)
+    scratch = [pltpu.VMEM(shape, blocks.dtype) for shape in ((2,) + piece, piece, piece)]
+    return call(fold_body, out, scratch + [pair_sems(3)], call_id, blocks)
+
+
+def trade(blocks, call_id):
+    count = blocks.shape[0]
+    out = jax.ShapeDtypeStruct(blocks.shape, blocks.dtype)
+    return call(functools.partial(trade_body, count), out, [pair_sems(count - 1)], call_id, blocks)
+
+
+def plane_peers(deep):
+    me = lax.axis_index("fsdp")
+    z, y = me // 2, me % 2
+    beside = 2 * z + 1 - y
+    ahead = [2 * ((z + step) % deep) + y for step in range(1, deep)]
+    behind = [2 * ((z + deep - step) % deep) + y for step in range(1, deep)]
+    return me, z, y, beside, ahead, behind
+
+
+def collect_body(arrays, deep, *refs):
+    owns, outs = refs[:arrays], refs[arrays : 2 * arrays]
+    sems = refs[2 * arrays]
+    me, z, y, beside, ahead, behind = plane_peers(deep)
+    meet("fsdp", [beside] + ahead)
+    every = 2 * deep - 1
+    along = []
+    copies = []
+    for at in range(arrays):
+        for step, peer in enumerate(ahead):
+            along.append(push("fsdp", peer, owns[at], outs[at].at[me], sems, at * every + step))
+        near = push("fsdp", beside, owns[at], outs[at].at[me], sems, at * every + deep - 1)
+        copies.append(near)
+        outs[at][me] = owns[at][...]
+    for at in range(arrays):
+        for step, origin in enumerate(behind):
+            along[at * (deep - 1) + step].wait_recv()
+            block = outs[at].at[origin]
+            copies.append(push("fsdp", beside, block, block, sems, at * every + deep + step))
+    for copy in along:
+        copy.wait_send()
+    for copy in copies:
+        copy.wait()
+
+
+def collect_all(owns, shards):
+    out = [jax.ShapeDtypeStruct((shards,) + own.shape, own.dtype) for own in owns]
+    deep = shards // 2
+    sems = pair_sems(len(owns) * (2 * deep - 1))
+    return call(functools.partial(collect_body, len(owns), deep), out, [sems], 5, *owns)
+
+
+def reduce_body(arrays, deep, *refs):
+    parts, outs = refs[:arrays], refs[arrays : 2 * arrays]
+    lands, arrivals = refs[2 * arrays : 3 * arrays], refs[3 * arrays : 4 * arrays]
+    sems = refs[4 * arrays]
+    me, z, y, beside, ahead, behind = plane_peers(deep)
+    meet("fsdp", [beside] + ahead)
+    every = 2 * deep - 1
+    near = []
+    far = []
+    order = list(range(1, deep)) + [0]
+    for at in range(arrays):
+        for step in order:
+            source = parts[at].at[2 * ((z + step) % deep) + 1 - y]
+            near.append(push("fsdp", beside, source, lands[at].at[step], sems, at * every + step))
+    for at in range(arrays):
+        for place, step in enumerate(order):
+            near[at * deep + place].wait_recv()
+            mine = parts[at][2 * ((z + step) % deep) + y].astype(jnp.float32)
+            total = mine + lands[at][step].astype(jnp.float32)
+            lands[at][step] = total.astype(jnp.bfloat16)
+            if step:
+                target = arrivals[at].at[step - 1]
+                sem_at = at * every + deep + step - 1
+                far.append(push("fsdp", ahead[step - 1], lands[at].at[step], target, sems, sem_at))
+    for at in range(arrays):
+        total = lands[at][0].astype(jnp.float32)
+        for step in range(deep - 1):
+            far[at * (deep - 1) + step].wait_recv()
+            total = total + arrivals[at][step].astype(jnp.float32)
+        outs[at][...] = total.astype(jnp.bfloat16)
+    for copy in near + far:
+        copy.wait_send()
+
+
+def reduce_all(parts):
+    shards = parts[0].shape[0]
+    deep = shards // 2
+    pieces = [part.shape[1:] for part in parts]
+    out = [jax.ShapeDtypeStruct(piece, jnp.bfloat16) for piece in pieces]
+    scratch = [pltpu.VMEM((deep,) + piece, jnp.bfloat16) for piece in pieces]
+    scratch += [pltpu.VMEM((deep - 1,) + piece, jnp.bfloat16) for piece in pieces]
+    scratch.append(pair_sems(len(parts) * (2 * deep - 1)))
+    return call(functools.partial(reduce_body, len(parts), deep), out, scratch, 6, *parts)
 
 
 def gather_group(rows):
-    return swap(rows, 0, same=True).reshape(-1, rows.shape[1])
+    return spread(rows, 0).reshape(-1, rows.shape[1])
 
 
 def scatter_group(partial):
     count = lax.axis_size("seq")
     rows = partial.astype(jnp.bfloat16).reshape(count, -1, partial.shape[1])
-    return swap(rows, 1, add=True)
+    return fold(rows, 1)
 
 
 def dot(left, right):
@@ -185,22 +317,36 @@
     lift_cut = lift_cut.reshape(LAYERS, w_in.shape[1], 2 * part_ff)
     gain_cut = gains.reshape(LAYERS * 2, -1).T
 
-    def collect(shard):
-        return lax.all_gather(shard, "fsdp", axis=0, tiled=True)
-
+    def fill(rows, height, width):
+        return jnp.pad(rows, ((0, height - rows.shape[0]), (0, width - rows.shape[1])))
+
+    near = shards == 8
+    unit_pad = -(-down_cut.shape[1] // 16) * 16 if spread_ff else down_cut.shape[1]
+    first_width = 3 * part_width + 64
+    owns = []
+    for layer_at in range(LAYERS):
+        first = qkv_cut[layer_at]
+        if layer_at == 0:
+            first = jnp.concatenate([first, gain_cut], axis=1)
+            first = fill(first, first.shape[0], first_width)
+        owns.append(first)
+        owns.append(jnp.concatenate([w_attn_out[layer_at], lift_cut[layer_at]], axis=1))
+        owns.append(fill(down_cut[layer_at], unit_pad, D))
+    if near:
+        full = collect_all(owns, shards)
+    else:
+        full = [lax.all_gather(own, "fsdp", axis=0, tiled=False) for own in owns]
     weights = []
     for layer_at in range(LAYERS):
-        first = [qkv_cut[layer_at]]
+        first, rest, down = full[3 * layer_at : 3 * layer_at + 3]
+        first = first.reshape(D, -1)
+        rest = rest.reshape(D, -1)
+        if spread_ff:
+            down = down[:, :unit].reshape(part_ff, D)
+        else:
+            down = lax.dynamic_slice_in_dim(down.reshape(FF, D), seq_at * part_ff, part_ff, 0)
         if layer_at == 0:
-            first.append(gain_cut)
-        rest = jnp.concatenate([w_attn_out[layer_at], lift_cut[layer_at]], axis=1)
-        first = collect(jnp.concatenate(first, axis=1))
-        rest = collect(rest)
-        down = collect(down_cut[layer_at])
-        if not spread_ff:
-            down = lax.dynamic_slice_in_dim(down, seq_at * part_ff, part_ff, 0)
-        if layer_at == 0:
-            gain_full = first[:, 3 * part_width :].T.astype(jnp.float32)
+            gain_full = first[:, 3 * part_width : 3 * part_width + 4].T.astype(jnp.float32)
         weights.append((first[:, : 3 * part_width], rest[:, :D], rest[:, D:], down))
     gain_full = gain_full.reshape(LAYERS, 2, 1, D)
 
@@ -228,7 +374,7 @@
             "hqk,hkd->qhd", probs.astype(jnp.bfloat16), v, preferred_element_type=jnp.float32
         )
         mixture = mixture.astype(jnp.bfloat16).reshape(group_rows, part_width)
-        mix_all = swap(mixture, 2, same=True)
+        mix_all = spread(mixture, 2)
         returned = lax.dynamic_slice_in_dim(mix_all, seq_at * local_rows, local_rows, 1)
         returned = returned.transpose(1, 0, 2).reshape(local_rows, D)
         stream = stream + dot(returned, proj_w)
@@ -292,7 +438,7 @@
                 grad_a.reshape(local_rows, seq_count, part_width),
             ]
         ).transpose(2, 0, 1, 3)
-        pair = swap(pair, 3)
+        pair = trade(pair, 3)
         grad_heads = (
             pair[:, 0].reshape(group_rows, part_heads, HEAD).transpose(1, 0, 2)
         )
@@ -333,17 +479,31 @@
         late = jnp.concatenate(
             [t_dot(normed_all, grad_qkv), gain_attn.T, gain_ffn.T], axis=1
         ).astype(jnp.bfloat16)
+        late = fill(late, D, first_width)
         down_grad = t_dot(gated, grad_y).astype(jnp.bfloat16)
-        if not spread_ff:
+        if spread_ff:
+            down_grad = jnp.pad(
+                down_grad.reshape(shards, unit, D), ((0, 0), (0, unit_pad - unit), (0, 0))
+            )
+        else:
             wide = jnp.zeros((FF, D), jnp.bfloat16)
             down_grad = lax.dynamic_update_slice_in_dim(wide, down_grad, seq_at * part_ff, 0)
-        sums = [
-            lax.psum_scatter(part, "fsdp", scatter_dimension=0, tiled=True)
-            for part in (down_grad, early, late)
+            down_grad = down_grad.reshape(shards, -1, D)
+        grads[layer_at] = [
+            down_grad,
+            early.reshape(shards, -1, D),
+            late.reshape(shards, -1, first_width),
         ]
-        grads[layer_at] = [
-            lax.all_gather(part, "seq", axis=0, tiled=False).astype(jnp.float32) for part in sums
-        ]
+
+    parts = grads[1] + grads[0]
+    if near:
+        sums = reduce_all(parts)
+    else:
+        sums = [lax.psum_scatter(part, "fsdp", scatter_dimension=0) for part in parts]
+    sums = [jnp.concatenate([sums[at + 3], sums[at]], axis=0) for at in range(3)]
+    sums = [spread(part, 7 + at).astype(jnp.float32) for at, part in enumerate(sums)]
+    sums = [part.reshape(seq_count, LAYERS, -1, part.shape[-1]) for part in sums]
+    grads = [[part[:, layer_at] for part in sums] for layer_at in range(LAYERS)]
 
     def whole(parts, blocks, width):
         parts = parts.reshape(seq_count, -1, blocks, width)
@@ -356,11 +516,11 @@
         lift = early[:, :, : 2 * part_ff]
         if spread_ff:
             out[2].append(whole(lift, 2 * shards, ff_rows // seq_count))
-            out[3].append(down.reshape(ff_rows, D))
+            out[3].append(down[:, :unit].reshape(ff_rows, D))
         else:
             out[2].append(whole(lift, 2, part_ff))
             out[3].append(jnp.sum(down, axis=0))
-        out[4].append(jnp.sum(late[:, :, 3 * part_width :], axis=0).T)
+        out[4].append(jnp.sum(late[:, :, 3 * part_width : 3 * part_width + 2], axis=0).T)
     return (block_out, gradient, *[jnp.stack(member) for member in out])
 
 

time: 676 us -> 500 us (0.74)
  blocking collectives: 215 us -> 0 us
  Pallas kernels: 174 us -> 330 us
  waiting for transfers between devices: 95.7 us -> 0 us
  between operations: 17.1 us -> 3.23 us
  local copies, waits for them, and re-layouts: 69.1 us -> 79.7 us
  other arithmetic: 36.4 us -> 27.4 us
    all_gather x10 -> x0, blocking collectives: 183 us -> none  [the longest x4 142 us: collect(): return lax.all_gather(shard, 'fsdp', axis=0, tiled=True)]
    pallas_call x16 -> x21, Pallas kernels: 174 us -> 330 us  [call(): pl.pallas_call(body, out_shape=out, in_specs=[space] * len(operands), out...]
    reduce_scatter x4 -> x0, waiting for transfers between devices: 94.8 us -> none  [on_device(): lax.psum_scatter(part, 'fsdp', scatter_dimension=0, tiled=True)]
    unnamed x1 -> x0, blocking collectives: 32.5 us -> none
    unnamed x189 -> x223, local copies, waits for them, and re-layouts: 21.2 us -> 28.6 us
  transfers between devices with their start and end apart: 8 -> 0, of which waited for: 3 -> 0; matrix products, arithmetic and copies ran while one was open for 19% -> 0% of each run, Pallas kernels for 18% -> 0%
where the time goes in v2:
time: 500 us; the launch traced here: 491 us
  Pallas kernels  330 us (66%)
  local copies, waits for them, and re-layouts  79.7 us (16%)
  matrix products  50.7 us (10%)
  other arithmetic  27.4 us (5%)
    pallas_call x21, Pallas kernels, call(): pl.pallas_call(body, out_shape=out, in_specs=[space] * len(operands), out...  330 us
    unnamed x223, local copies, waits for them, and re-layouts  28.6 us

profile of v2, /device:TPU:0, one launch (start us, length us, event | category | flops | bytes accessed | tf_op | source)
XLA Modules:
  0.0 490.7 jit_solution(12138197164433378789)
XLA Ops:
  9.0 9.6 %shard_map.144 = bf16[4,128,768]{2,1,0:T(8,128)(2,1)S(1)} custom-call(bf16[128,768]{1,0:T(8,128)(2,1)S(1)} %copy-done.8), custom_call_target="tpu_custom_call" | custom-call | tf_op jit(solution)/shard_map/pallas_call | solution.py:128
  20.3 2.9 reshape.507
  24.7 3.1 copy.153
  30.0 98.5 %shard_map.135 = (bf16[8,96,640]{2,1,0:T(8,128)(2,1)S(1)}, bf16[8,96,1344]{2,1,0:T(8,128)(2,1)S(1)}, bf16[8,48,768]{2,1,0:T(8,128)(2,1)S(1)}, bf16[8,96,576]{2,1...) custom-call(bf16[96,640]{1,0:T(8,128)(2,1)S(1)} %fusion.92.refs_0_, ...), custom_call_target="tpu_custom_call" | custom-call | tf_op jit(solution)/shard_map/pallas_call | solution.py:128
  138.9 7.7 %shard_map.136 = bf16[4,128,768]{2,1,0:T(8,128)(2,1)S(1)} custom-call(bf16[128,768]{1,0:T(8,128)(2,1)S(1)} %fusion.51.own_ref), custom_call_target="tpu_custom_call" | custom-call | tf_op jit(solution)/shard_map/pallas_call | solution.py:128
  146.6 2.5 copy.162
  153.8 2.9 fusion.127
  159.4 9.8 %shard_map.137 = bf16[4,512,192]{2,1,0:T(8,128)(2,1)S(1)} custom-call(bf16[512,192]{1,0:T(8,128)(2,1)S(1)} %copy.160.own_ref), custom_call_target="tpu_custom_call" | custom-call | tf_op jit(solution)/shard_map/pallas_call | solution.py:128
  171.5 8.3 %shard_map.138 = bf16[4,128,768]{2,1,0:T(8,128)(2,1)S(1)} custom-call(bf16[128,768]{1,0:T(8,128)(2,1)S(1)} %multiply_convert_fusion.6.own_ref), custom_call_target="tpu_custom_call" | custom-call | tf_op jit(solution)/shard_map/pallas_call | solution.py:128
  187.4 8.7 %shard_map.139 = f32[128,768]{1,0:T(8,128)S(1)} custom-call(bf16[4,128,768]{2,1,0:T(8,128)(2,1)S(1)} %bitcast.306), custom_call_target="tpu_custom_call" | custom-call | tf_op jit(solution)/shard_map/pallas_call | solution.py:128
  197.7 7.8 %shard_map.140 = bf16[4,128,768]{2,1,0:T(8,128)(2,1)S(1)} custom-call(bf16[128,768]{1,0:T(8,128)(2,1)S(1)} %multiply_convert_fusion.5.own_ref), custom_call_target="tpu_custom_call" | custom-call | tf_op jit(solution)/shard_map/pallas_call | solution.py:128
  208.4 4.1 fusion.129
  212.5 3.0 convolution_convert_fusion.18
  216.5 9.8 %shard_map.141 = bf16[4,512,192]{2,1,0:T(8,128)(2,1)S(1)} custom-call(bf16[512,192]{1,0:T(8,128)(2,1)S(1)} %copy.164.own_ref), custom_call_target="tpu_custom_call" | custom-call | tf_op jit(solution)/shard_map/pallas_call | solution.py:128
  229.4 8.3 %shard_map.142 = bf16[4,128,768]{2,1,0:T(8,128)(2,1)S(1)} custom-call(bf16[128,768]{1,0:T(8,128)(2,1)S(1)} %multiply_convert_fusion.4.own_ref), custom_call_target="tpu_custom_call" | custom-call | tf_op jit(solution)/shard_map/pallas_call | solution.py:128
  247.7 3.0 convolution_convert_fusion.1
  251.6 8.7 %shard_map.145 = f32[128,768]{1,0:T(8,128)S(1)} custom-call(bf16[4,128,768]{2,1,0:T(8,128)(2,1)S(1)} %bitcast.303), custom_call_target="tpu_custom_call" | custom-call | tf_op jit(solution)/shard_map/pallas_call | solution.py:128
  261.8 8.2 %shard_map.143 = f32[128,768]{1,0:T(8,128)S(1)} custom-call(bf16[4,128,768]{2,1,0:T(8,128)(2,1)S(1)} %bitcast.304), custom_call_target="tpu_custom_call" | custom-call | tf_op jit(solution)/shard_map/pallas_call | solution.py:128
  272.2 7.3 %shard_map.146 = bf16[4,2,128,192]{3,2,1,0:T(8,128)(2,1)S(1)} custom-call(bf16[4,2,128,192]{3,2,1,0:T(8,128)(2,1)S(1)} %maximum_bitcast_fusion.own_ref), custom_call_target="tpu_custom_call" | custom-call | tf_op jit(solution)/shard_map/pallas_call | solution.py:128
  281.8 2.6 fusion.10
  291.4 9.0 %shard_map.147 = f32[128,768]{1,0:T(8,128)S(1)} custom-call(bf16[4,128,768]{2,1,0:T(8,128)(2,1)S(1)} %bitcast.301), custom_call_target="tpu_custom_call" | custom-call | tf_op jit(solution)/shard_map/pallas_call | solution.py:128
  304.9 7.7 %shard_map.148 = bf16[4,128,768]{2,1,0:T(8,128)(2,1)S(1)} custom-call(bf16[128,768]{1,0:T(8,128)(2,1)S(1)} %get-tuple-element.68.own_ref), custom_call_target="tpu_custom_call" | custom-call | tf_op jit(solution)/shard_map/pallas_call | solution.py:128
  317.5 3.2 convolution_convert_fusion
  321.6 8.7 %shard_map.149 = f32[128,768]{1,0:T(8,128)S(1)} custom-call(bf16[4,128,768]{2,1,0:T(8,128)(2,1)S(1)} %bitcast.305), custom_call_target="tpu_custom_call" | custom-call | tf_op jit(solution)/shard_map/pallas_call | solution.py:128
  332.8 7.3 %shard_map.150 = bf16[4,2,128,192]{3,2,1,0:T(8,128)(2,1)S(1)} custom-call(bf16[4,2,128,192]{3,2,1,0:T(8,128)(2,1)S(1)} %maximum_bitcast_fusion.1.own_ref), custom_call_target="tpu_custom_call" | custom-call | tf_op jit(solution)/shard_map/pallas_call | solution.py:128
  343.4 2.6 fusion.11
  353.9 9.0 %shard_map.151 = f32[128,768]{1,0:T(8,128)S(1)} custom-call(bf16[4,128,768]{2,1,0:T(8,128)(2,1)S(1)} %bitcast.302), custom_call_target="tpu_custom_call" | custom-call | tf_op jit(solution)/shard_map/pallas_call | solution.py:128
  369.4 68.6 %shard_map.152 = (bf16[48,768]{1,0:T(8,128)(2,1)S(1)}, bf16[96,768]{1,0:T(8,128)(2,1)S(1)}, bf16[96,640]{1,0:T(8,128)(2,1)S(1)}, bf16[48,768]{1,0:T(8,128)(2,1)S...) custom-call(bf16[8,48,768]{2,1,0:T(8,128)(2,1)S(1)} %copy-done.2, ...), custom_call_target="tpu_custom_call" | custom-call | tf_op jit(solution)/shard_map/pallas_call | solution.py:128
  438.1 6.6 %shard_map.155 = bf16[4,96,768]{2,1,0:T(8,128)(2,1)S(1)} custom-call(bf16[96,768]{1,0:T(8,128)(2,1)S(1)} %pad_maximum_fusion.14.own_ref), custom_call_target="tpu_custom_call" | custom-call | tf_op jit(solution)/shard_map/pallas_call | solution.py:128
  446.1 9.4 %shard_map.153 = bf16[4,192,640]{2,1,0:T(8,128)(2,1)S(1)} custom-call(bf16[192,640]{1,0:T(8,128)(2,1)S(1)} %pad_maximum_fusion.13.own_ref), custom_call_target="tpu_custom_call" | custom-call | tf_op jit(solution)/shard_map/pallas_call | solution.py:128
  455.5 10.6 %shard_map.154 = bf16[4,192,768]{2,1,0:T(8,128)(2,1)S(1)} custom-call(bf16[192,768]{1,0:T(8,128)(2,1)S(1)} %pad_maximum_fusion.10.own_ref), custom_call_target="tpu_custom_call" | custom-call | tf_op jit(solution)/shard_map/pallas_call | solution.py:128
  479.5 2.9 pad_maximum_fusion.1
  (418 shorter events, 125.2 us)
Async XLA Ops:
  3.1 132.0 %copy-start.71 = (f32[128]{0:T(128)}, f32[128]{0:T(128)S(1)}, u32[]{:S(2)}) copy-start(f32[128]{0:T(128)S(1)} %broadcast_multiply_fusion.13) | copy-start | bytes 1540
  4.3 130.8 %copy-start.84 = (f32[128]{0:T(128)}, f32[128]{0:T(128)S(1)}, u32[]{:S(2)}) copy-start(f32[128]{0:T(128)S(1)} %fusion.99) | copy-start | bytes 1540
  29.9 105.2 %copy-start.22 = (bf16[128,768]{1,0:T(8,128)(2,1)S(1)}, bf16[128,768]{1,0:T(8,128)(2,1)}, u32[]{:S(2)}) copy-start(bf16[128,768]{1,0:T(8,128)(2,1)} %param.8) | copy-start | bytes 589828
  132.0 17.0 %copy-start.10 = (bf16[8,96,640]{2,1,0:T(8,128)(2,1)}, bf16[8,96,640]{2,1,0:T(8,128)(2,1)S(1)}, u32[]{:S(2)}) copy-start(bf16[8,96,640]{2,1,0:T(8,128)(2,1)S(1)} %get-tuple-element.19) | copy-start | bytes 2949124
  159.2 10.2 %copy-start.23 = (bf16[128,768]{1,0:T(8,128)(2,1)S(1)}, bf16[128,768]{1,0:T(8,128)(2,1)}, u32[]{:S(2)}) copy-start(bf16[128,768]{1,0:T(8,128)(2,1)} %param.8) | copy-start | bytes 589828
  171.1 25.0 %copy-start.18 = (f32[128,768]{1,0:T(8,128)}, f32[128,768]{1,0:T(8,128)S(1)}, u32[]{:S(2)}) copy-start(f32[128,768]{1,0:T(8,128)S(1)} %get-tuple-element.148) | copy-start | bytes 1179652
  171.1 9.9 %copy-start.74 = (f32[128]{0:T(128)}, f32[128]{0:T(128)S(1)}, u32[]{:S(2)}) copy-start(f32[128]{0:T(128)S(1)} %broadcast_multiply_fusion.12) | copy-start | bytes 1540
  171.3 9.7 %copy-start.96 = (f32[128]{0:T(128)}, f32[128]{0:T(128)S(1)}, u32[]{:S(2)}) copy-start(f32[128]{0:T(128)S(1)} %multiply_reduce_fusion.10) | copy-start | bytes 1540
  171.4 9.6 %copy-start.86 = (f32[128]{0:T(128)}, f32[128]{0:T(128)S(1)}, u32[]{:S(2)}) copy-start(f32[128]{0:T(128)S(1)} %fusion.100) | copy-start | bytes 1540
  196.1 9.5 %copy-start.32 = (bf16[576,768]{1,0:T(8,128)(2,1)S(1)}, bf16[576,768]{1,0:T(8,128)(2,1)}, u32[]{:S(2)}) copy-start(bf16[576,768]{1,0:T(8,128)(2,1)} %copy.162) | copy-start | bytes 2654212
  196.2 30.9 %copy-start.16 = (f32[128,768]{1,0:T(8,128)}, f32[128,768]{1,0:T(8,128)S(1)}, u32[]{:S(2)}) copy-start(f32[128,768]{1,0:T(8,128)S(1)} %get-tuple-element.77) | copy-start | bytes 1179652
  250.7 9.6 %copy-start.21 = (f32[128,768]{1,0:T(8,128)S(1)}, f32[128,768]{1,0:T(8,128)}, u32[]{:S(2)}) copy-start(f32[128,768]{1,0:T(8,128)} %copy-done.20) | copy-start | bytes 1179652
  250.7 9.6 %copy-start.83 = (f32[128]{0:T(128)S(1)}, f32[128]{0:T(128)}, u32[]{:S(2)}) copy-start(f32[128]{0:T(128)} %copy-done.82) | copy-start | bytes 1540
  250.7 9.6 %copy-start.91 = (f32[128]{0:T(128)S(1)}, f32[128]{0:T(128)}, u32[]{:S(2)}) copy-start(f32[128]{0:T(128)} %copy-done.90) | copy-start | bytes 1540
  251.5 9.6 %copy-start.68 = (bf16[288,768]{1,0:T(8,128)(2,1)S(1)}, bf16[288,768]{1,0:T(8,128)(2,1)}, u32[]{:S(2)}) copy-start(bf16[288,768]{1,0:T(8,128)(2,1)} %reshape.526) | copy-start | bytes 1327108
  290.7 9.6 %copy-start.17 = (f32[128,768]{1,0:T(8,128)S(1)}, f32[128,768]{1,0:T(8,128)}, u32[]{:S(2)}) copy-start(f32[128,768]{1,0:T(8,128)} %copy-done.16) | copy-start | bytes 1179652
  290.8 9.6 %copy-start.77 = (f32[128]{0:T(128)S(1)}, f32[128]{0:T(128)}, u32[]{:S(2)}) copy-start(f32[128]{0:T(128)} %copy-done.76) | copy-start | bytes 1540
  290.8 9.6 %copy-start.89 = (f32[128]{0:T(128)S(1)}, f32[128]{0:T(128)}, u32[]{:S(2)}) copy-start(f32[128]{0:T(128)} %copy-done.88) | copy-start | bytes 1540
  291.4 9.3 %copy-start.99 = (f32[128]{0:T(128)S(1)}, f32[128]{0:T(128)}, u32[]{:S(2)}) copy-start(f32[128]{0:T(128)} %copy-done.98) | copy-start | bytes 1540
  291.4 9.5 %copy-start.38 = (f32[128,768]{1,0:T(8,128)S(1)}, f32[128,768]{1,0:T(8,128)}, u32[]{:S(2)}) copy-start(f32[128,768]{1,0:T(8,128)} %copy-done.37) | copy-start | bytes 1179652
  303.4 9.2 %copy-start.66 = (bf16[288,768]{1,0:T(8,128)(2,1)S(1)}, bf16[288,768]{1,0:T(8,128)(2,1)}, u32[]{:S(2)}) copy-start(bf16[288,768]{1,0:T(8,128)(2,1)} %reshape.518) | copy-start | bytes 1327108
  320.7 9.6 %copy-start.19 = (f32[128,768]{1,0:T(8,128)S(1)}, f32[128,768]{1,0:T(8,128)}, u32[]{:S(2)}) copy-start(f32[128,768]{1,0:T(8,128)} %copy-done.18) | copy-start | bytes 1179652
  320.7 9.6 %copy-start.75 = (f32[128]{0:T(128)S(1)}, f32[128]{0:T(128)}, u32[]{:S(2)}) copy-start(f32[128]{0:T(128)} %copy-done.74) | copy-start | bytes 1540
  320.7 9.6 %copy-start.87 = (f32[128]{0:T(128)S(1)}, f32[128]{0:T(128)}, u32[]{:S(2)}) copy-start(f32[128]{0:T(128)} %copy-done.86) | copy-start | bytes 1540
  321.6 9.3 %copy-start.33 = (f32[128,768]{1,0:T(8,128)S(1)}, f32[128,768]{1,0:T(8,128)}, u32[]{:S(2)}) copy-start(f32[128,768]{1,0:T(8,128)} %get-tuple-element.69) | copy-start | bytes 1179652
  353.2 9.7 %copy-start.24 = (bf16[128,768]{1,0:T(8,128)(2,1)S(1)}, bf16[128,768]{1,0:T(8,128)(2,1)}, u32[]{:S(2)}) copy-start(bf16[128,768]{1,0:T(8,128)(2,1)} %param.8) | copy-start | bytes 589828
  353.2 9.7 %copy-start.72 = (f32[128]{0:T(128)S(1)}, f32[128]{0:T(128)}, u32[]{:S(2)}) copy-start(f32[128]{0:T(128)} %copy-done.71) | copy-start | bytes 1540
  353.2 9.9 %copy-start.95 = (f32[128]{0:T(128)S(1)}, f32[128]{0:T(128)}, u32[]{:S(2)}) copy-start(f32[128]{0:T(128)} %copy-done.94) | copy-start | bytes 1540
  353.2 9.9 %copy-start.85 = (f32[128]{0:T(128)S(1)}, f32[128]{0:T(128)}, u32[]{:S(2)}) copy-start(f32[128]{0:T(128)} %copy-done.84) | copy-start | bytes 1540
  353.9 9.5 %copy-start.34 = (f32[128,768]{1,0:T(8,128)S(1)}, f32[128,768]{1,0:T(8,128)}, u32[]{:S(2)}) copy-start(f32[128,768]{1,0:T(8,128)} %get-tuple-element.69) | copy-start | bytes 1179652
  353.9 9.5 %copy-start.36 = (f32[128,768]{1,0:T(8,128)S(1)}, f32[128,768]{1,0:T(8,128)}, u32[]{:S(2)}) copy-start(f32[128,768]{1,0:T(8,128)} %copy-done.35) | copy-start | bytes 1179652
  353.9 9.5 %copy-start.93 = (f32[128]{0:T(128)S(1)}, f32[128]{0:T(128)}, u32[]{:S(2)}) copy-start(f32[128]{0:T(128)} %copy-done.92) | copy-start | bytes 1540
  (74 other events, 231.3 us)

commit v3 on v2

--- a/solution.py
+++ b/solution.py
@@ -176,17 +176,23 @@
     every = 2 * deep - 1
     along = []
     copies = []
-    for at in range(arrays):
+
+    def issue(at):
         for step, peer in enumerate(ahead):
             along.append(push("fsdp", peer, owns[at], outs[at].at[me], sems, at * every + step))
         near = push("fsdp", beside, owns[at], outs[at].at[me], sems, at * every + deep - 1)
         copies.append(near)
+
+    for at in range(min(2, arrays)):
+        issue(at)
+    for at in range(arrays):
         outs[at][me] = owns[at][...]
-    for at in range(arrays):
         for step, origin in enumerate(behind):
             along[at * (deep - 1) + step].wait_recv()
             block = outs[at].at[origin]
             copies.append(push("fsdp", beside, block, block, sems, at * every + deep + step))
+        if at + 2 < arrays:
+            issue(at + 2)
     for copy in along:
         copy.wait_send()
     for copy in copies:
@@ -210,10 +216,14 @@
     near = []
     far = []
     order = list(range(1, deep)) + [0]
-    for at in range(arrays):
+
+    def issue(at):
         for step in order:
             source = parts[at].at[2 * ((z + step) % deep) + 1 - y]
             near.append(push("fsdp", beside, source, lands[at].at[step], sems, at * every + step))
+
+    for at in range(min(3, arrays)):
+        issue(at)
     for at in range(arrays):
         for place, step in enumerate(order):
             near[at * deep + place].wait_recv()
@@ -224,6 +234,8 @@
                 target = arrivals[at].at[step - 1]
                 sem_at = at * every + deep + step - 1
                 far.append(push("fsdp", ahead[step - 1], lands[at].at[step], target, sems, sem_at))
+        if at + 3 < arrays:
+            issue(at + 3)
     for at in range(arrays):
         total = lands[at][0].astype(jnp.float32)
         for step in range(deep - 1):

time: 500 us -> 505 us (1.010)
  no operation moved by 1% of the time
where the time goes in v3:
time: 505 us; the launch traced here: 496 us
  Pallas kernels  335 us (66%)
  local copies, waits for them, and re-layouts  79.7 us (16%)
  matrix products  50.7 us (10%)
  other arithmetic  27.4 us (5%)
    pallas_call x21, Pallas kernels, call(): pl.pallas_call(body, out_shape=out, in_specs=[space] * len(operands), out...  335 us
    unnamed x223, local copies, waits for them, and re-layouts  28.6 us

profile of v3, /device:TPU:0, one launch (start us, length us, event | category | flops | bytes accessed | tf_op | source)
XLA Modules:
  0.0 495.6 jit_solution(6479303832422135459)
XLA Ops:
  9.0 9.6 %shard_map.144 = bf16[4,128,768]{2,1,0:T(8,128)(2,1)S(1)} custom-call(bf16[128,768]{1,0:T(8,128)(2,1)S(1)} %copy-done.8), custom_call_target="tpu_custom_call" | custom-call | tf_op jit(solution)/shard_map/pallas_call | solution.py:128
  20.3 2.9 reshape.507
  24.7 3.1 copy.153
  30.0 95.8 %shard_map.135 = (bf16[8,96,640]{2,1,0:T(8,128)(2,1)S(1)}, bf16[8,96,1344]{2,1,0:T(8,128)(2,1)S(1)}, bf16[8,48,768]{2,1,0:T(8,128)(2,1)S(1)}, bf16[8,96,576]{2,1...) custom-call(bf16[96,640]{1,0:T(8,128)(2,1)S(1)} %fusion.92.refs_0_, ...), custom_call_target="tpu_custom_call" | custom-call | tf_op jit(solution)/shard_map/pallas_call | solution.py:128
  136.2 7.7 %shard_map.136 = bf16[4,128,768]{2,1,0:T(8,128)(2,1)S(1)} custom-call(bf16[128,768]{1,0:T(8,128)(2,1)S(1)} %fusion.51.own_ref), custom_call_target="tpu_custom_call" | custom-call | tf_op jit(solution)/shard_map/pallas_call | solution.py:128
  143.9 2.5 copy.162
  151.1 2.9 fusion.127
  156.7 9.8 %shard_map.137 = bf16[4,512,192]{2,1,0:T(8,128)(2,1)S(1)} custom-call(bf16[512,192]{1,0:T(8,128)(2,1)S(1)} %copy.160.own_ref), custom_call_target="tpu_custom_call" | custom-call | tf_op jit(solution)/shard_map/pallas_call | solution.py:128
  168.8 8.3 %shard_map.138 = bf16[4,128,768]{2,1,0:T(8,128)(2,1)S(1)} custom-call(bf16[128,768]{1,0:T(8,128)(2,1)S(1)} %multiply_convert_fusion.6.own_ref), custom_call_target="tpu_custom_call" | custom-call | tf_op jit(solution)/shard_map/pallas_call | solution.py:128
  184.7 8.7 %shard_map.139 = f32[128,768]{1,0:T(8,128)S(1)} custom-call(bf16[4,128,768]{2,1,0:T(8,128)(2,1)S(1)} %bitcast.306), custom_call_target="tpu_custom_call" | custom-call | tf_op jit(solution)/shard_map/pallas_call | solution.py:128
  195.0 7.8 %shard_map.140 = bf16[4,128,768]{2,1,0:T(8,128)(2,1)S(1)} custom-call(bf16[128,768]{1,0:T(8,128)(2,1)S(1)} %multiply_convert_fusion.5.own_ref), custom_call_target="tpu_custom_call" | custom-call | tf_op jit(solution)/shard_map/pallas_call | solution.py:128
  205.7 4.1 fusion.129
  209.8 3.0 convolution_convert_fusion.18
  213.8 9.8 %shard_map.141 = bf16[4,512,192]{2,1,0:T(8,128)(2,1)S(1)} custom-call(bf16[512,192]{1,0:T(8,128)(2,1)S(1)} %copy.164.own_ref), custom_call_target="tpu_custom_call" | custom-call | tf_op jit(solution)/shard_map/pallas_call | solution.py:128
  226.7 8.3 %shard_map.142 = bf16[4,128,768]{2,1,0:T(8,128)(2,1)S(1)} custom-call(bf16[128,768]{1,0:T(8,128)(2,1)S(1)} %multiply_convert_fusion.4.own_ref), custom_call_target="tpu_custom_call" | custom-call | tf_op jit(solution)/shard_map/pallas_call | solution.py:128
  245.0 3.0 convolution_convert_fusion.1
  248.9 8.7 %shard_map.145 = f32[128,768]{1,0:T(8,128)S(1)} custom-call(bf16[4,128,768]{2,1,0:T(8,128)(2,1)S(1)} %bitcast.303), custom_call_target="tpu_custom_call" | custom-call | tf_op jit(solution)/shard_map/pallas_call | solution.py:128
  259.1 8.2 %shard_map.143 = f32[128,768]{1,0:T(8,128)S(1)} custom-call(bf16[4,128,768]{2,1,0:T(8,128)(2,1)S(1)} %bitcast.304), custom_call_target="tpu_custom_call" | custom-call | tf_op jit(solution)/shard_map/pallas_call | solution.py:128
  269.5 7.3 %shard_map.146 = bf16[4,2,128,192]{3,2,1,0:T(8,128)(2,1)S(1)} custom-call(bf16[4,2,128,192]{3,2,1,0:T(8,128)(2,1)S(1)} %maximum_bitcast_fusion.own_ref), custom_call_target="tpu_custom_call" | custom-call | tf_op jit(solution)/shard_map/pallas_call | solution.py:128
  279.2 2.6 fusion.10
  288.7 9.0 %shard_map.147 = f32[128,768]{1,0:T(8,128)S(1)} custom-call(bf16[4,128,768]{2,1,0:T(8,128)(2,1)S(1)} %bitcast.301), custom_call_target="tpu_custom_call" | custom-call | tf_op jit(solution)/shard_map/pallas_call | solution.py:128
  302.2 7.7 %shard_map.148 = bf16[4,128,768]{2,1,0:T(8,128)(2,1)S(1)} custom-call(bf16[128,768]{1,0:T(8,128)(2,1)S(1)} %get-tuple-element.68.own_ref), custom_call_target="tpu_custom_call" | custom-call | tf_op jit(solution)/shard_map/pallas_call | solution.py:128
  314.8 3.2 convolution_convert_fusion
  318.9 8.7 %shard_map.149 = f32[128,768]{1,0:T(8,128)S(1)} custom-call(bf16[4,128,768]{2,1,0:T(8,128)(2,1)S(1)} %bitcast.305), custom_call_target="tpu_custom_call" | custom-call | tf_op jit(solution)/shard_map/pallas_call | solution.py:128
  330.2 7.3 %shard_map.150 = bf16[4,2,128,192]{3,2,1,0:T(8,128)(2,1)S(1)} custom-call(bf16[4,2,128,192]{3,2,1,0:T(8,128)(2,1)S(1)} %maximum_bitcast_fusion.1.own_ref), custom_call_target="tpu_custom_call" | custom-call | tf_op jit(solution)/shard_map/pallas_call | solution.py:128
  340.7 2.6 fusion.11
  351.2 9.0 %shard_map.151 = f32[128,768]{1,0:T(8,128)S(1)} custom-call(bf16[4,128,768]{2,1,0:T(8,128)(2,1)S(1)} %bitcast.302), custom_call_target="tpu_custom_call" | custom-call | tf_op jit(solution)/shard_map/pallas_call | solution.py:128
  366.7 76.2 %shard_map.152 = (bf16[48,768]{1,0:T(8,128)(2,1)S(1)}, bf16[96,768]{1,0:T(8,128)(2,1)S(1)}, bf16[96,640]{1,0:T(8,128)(2,1)S(1)}, bf16[48,768]{1,0:T(8,128)(2,1)S...) custom-call(bf16[8,48,768]{2,1,0:T(8,128)(2,1)S(1)} %copy-done.2, ...), custom_call_target="tpu_custom_call" | custom-call | tf_op jit(solution)/shard_map/pallas_call | solution.py:128
  443.0 6.6 %shard_map.155 = bf16[4,96,768]{2,1,0:T(8,128)(2,1)S(1)} custom-call(bf16[96,768]{1,0:T(8,128)(2,1)S(1)} %pad_maximum_fusion.14.own_ref), custom_call_target="tpu_custom_call" | custom-call | tf_op jit(solution)/shard_map/pallas_call | solution.py:128
  451.0 9.4 %shard_map.153 = bf16[4,192,640]{2,1,0:T(8,128)(2,1)S(1)} custom-call(bf16[192,640]{1,0:T(8,128)(2,1)S(1)} %pad_maximum_fusion.13.own_ref), custom_call_target="tpu_custom_call" | custom-call | tf_op jit(solution)/shard_map/pallas_call | solution.py:128
  460.4 10.6 %shard_map.154 = bf16[4,192,768]{2,1,0:T(8,128)(2,1)S(1)} custom-call(bf16[192,768]{1,0:T(8,128)(2,1)S(1)} %pad_maximum_fusion.10.own_ref), custom_call_target="tpu_custom_call" | custom-call | tf_op jit(solution)/shard_map/pallas_call | solution.py:128
  484.5 2.9 pad_maximum_fusion.1
  (418 shorter events, 125.2 us)
Async XLA Ops:
  3.1 129.3 %copy-start.71 = (f32[128]{0:T(128)}, f32[128]{0:T(128)S(1)}, u32[]{:S(2)}) copy-start(f32[128]{0:T(128)S(1)} %broadcast_multiply_fusion.13) | copy-start | bytes 1540
  4.3 128.1 %copy-start.84 = (f32[128]{0:T(128)}, f32[128]{0:T(128)S(1)}, u32[]{:S(2)}) copy-start(f32[128]{0:T(128)S(1)} %fusion.99) | copy-start | bytes 1540
  29.9 102.5 %copy-start.22 = (bf16[128,768]{1,0:T(8,128)(2,1)S(1)}, bf16[128,768]{1,0:T(8,128)(2,1)}, u32[]{:S(2)}) copy-start(bf16[128,768]{1,0:T(8,128)(2,1)} %param.8) | copy-start | bytes 589828
  129.4 17.0 %copy-start.10 = (bf16[8,96,640]{2,1,0:T(8,128)(2,1)}, bf16[8,96,640]{2,1,0:T(8,128)(2,1)S(1)}, u32[]{:S(2)}) copy-start(bf16[8,96,640]{2,1,0:T(8,128)(2,1)S(1)} %get-tuple-element.19) | copy-start | bytes 2949124
  156.5 10.2 %copy-start.23 = (bf16[128,768]{1,0:T(8,128)(2,1)S(1)}, bf16[128,768]{1,0:T(8,128)(2,1)}, u32[]{:S(2)}) copy-start(bf16[128,768]{1,0:T(8,128)(2,1)} %param.8) | copy-start | bytes 589828
  168.4 25.0 %copy-start.18 = (f32[128,768]{1,0:T(8,128)}, f32[128,768]{1,0:T(8,128)S(1)}, u32[]{:S(2)}) copy-start(f32[128,768]{1,0:T(8,128)S(1)} %get-tuple-element.148) | copy-start | bytes 1179652
  168.5 9.9 %copy-start.74 = (f32[128]{0:T(128)}, f32[128]{0:T(128)S(1)}, u32[]{:S(2)}) copy-start(f32[128]{0:T(128)S(1)} %broadcast_multiply_fusion.12) | copy-start | bytes 1540
  168.7 9.7 %copy-start.96 = (f32[128]{0:T(128)}, f32[128]{0:T(128)S(1)}, u32[]{:S(2)}) copy-start(f32[128]{0:T(128)S(1)} %multiply_reduce_fusion.10) | copy-start | bytes 1540
  168.7 9.6 %copy-start.86 = (f32[128]{0:T(128)}, f32[128]{0:T(128)S(1)}, u32[]{:S(2)}) copy-start(f32[128]{0:T(128)S(1)} %fusion.100) | copy-start | bytes 1540
  193.4 9.5 %copy-start.32 = (bf16[576,768]{1,0:T(8,128)(2,1)S(1)}, bf16[576,768]{1,0:T(8,128)(2,1)}, u32[]{:S(2)}) copy-start(bf16[576,768]{1,0:T(8,128)(2,1)} %copy.162) | copy-start | bytes 2654212
  193.5 30.9 %copy-start.16 = (f32[128,768]{1,0:T(8,128)}, f32[128,768]{1,0:T(8,128)S(1)}, u32[]{:S(2)}) copy-start(f32[128,768]{1,0:T(8,128)S(1)} %get-tuple-element.77) | copy-start | bytes 1179652
  248.0 9.6 %copy-start.21 = (f32[128,768]{1,0:T(8,128)S(1)}, f32[128,768]{1,0:T(8,128)}, u32[]{:S(2)}) copy-start(f32[128,768]{1,0:T(8,128)} %copy-done.20) | copy-start | bytes 1179652
  248.0 9.6 %copy-start.83 = (f32[128]{0:T(128)S(1)}, f32[128]{0:T(128)}, u32[]{:S(2)}) copy-start(f32[128]{0:T(128)} %copy-done.82) | copy-start | bytes 1540
  248.0 9.6 %copy-start.91 = (f32[128]{0:T(128)S(1)}, f32[128]{0:T(128)}, u32[]{:S(2)}) copy-start(f32[128]{0:T(128)} %copy-done.90) | copy-start | bytes 1540
  248.9 9.6 %copy-start.68 = (bf16[288,768]{1,0:T(8,128)(2,1)S(1)}, bf16[288,768]{1,0:T(8,128)(2,1)}, u32[]{:S(2)}) copy-start(bf16[288,768]{1,0:T(8,128)(2,1)} %reshape.526) | copy-start | bytes 1327108
  288.1 9.6 %copy-start.17 = (f32[128,768]{1,0:T(8,128)S(1)}, f32[128,768]{1,0:T(8,128)}, u32[]{:S(2)}) copy-start(f32[128,768]{1,0:T(8,128)} %copy-done.16) | copy-start | bytes 1179652
  288.1 9.6 %copy-start.77 = (f32[128]{0:T(128)S(1)}, f32[128]{0:T(128)}, u32[]{:S(2)}) copy-start(f32[128]{0:T(128)} %copy-done.76) | copy-start | bytes 1540
  288.1 9.6 %copy-start.89 = (f32[128]{0:T(128)S(1)}, f32[128]{0:T(128)}, u32[]{:S(2)}) copy-start(f32[128]{0:T(128)} %copy-done.88) | copy-start | bytes 1540
  288.7 9.3 %copy-start.99 = (f32[128]{0:T(128)S(1)}, f32[128]{0:T(128)}, u32[]{:S(2)}) copy-start(f32[128]{0:T(128)} %copy-done.98) | copy-start | bytes 1540
  288.7 9.5 %copy-start.38 = (f32[128,768]{1,0:T(8,128)S(1)}, f32[128,768]{1,0:T(8,128)}, u32[]{:S(2)}) copy-start(f32[128,768]{1,0:T(8,128)} %copy-done.37) | copy-start | bytes 1179652
  300.8 9.2 %copy-start.66 = (bf16[288,768]{1,0:T(8,128)(2,1)S(1)}, bf16[288,768]{1,0:T(8,128)(2,1)}, u32[]{:S(2)}) copy-start(bf16[288,768]{1,0:T(8,128)(2,1)} %reshape.518) | copy-start | bytes 1327108
  318.0 9.6 %copy-start.19 = (f32[128,768]{1,0:T(8,128)S(1)}, f32[128,768]{1,0:T(8,128)}, u32[]{:S(2)}) copy-start(f32[128,768]{1,0:T(8,128)} %copy-done.18) | copy-start | bytes 1179652
  318.0 9.6 %copy-start.75 = (f32[128]{0:T(128)S(1)}, f32[128]{0:T(128)}, u32[]{:S(2)}) copy-start(f32[128]{0:T(128)} %copy-done.74) | copy-start | bytes 1540
  318.0 9.6 %copy-start.87 = (f32[128]{0:T(128)S(1)}, f32[128]{0:T(128)}, u32[]{:S(2)}) copy-start(f32[128]{0:T(128)} %copy-done.86) | copy-start | bytes 1540
  318.9 9.3 %copy-start.33 = (f32[128,768]{1,0:T(8,128)S(1)}, f32[128,768]{1,0:T(8,128)}, u32[]{:S(2)}) copy-start(f32[128,768]{1,0:T(8,128)} %get-tuple-element.69) | copy-start | bytes 1179652
  350.5 9.7 %copy-start.24 = (bf16[128,768]{1,0:T(8,128)(2,1)S(1)}, bf16[128,768]{1,0:T(8,128)(2,1)}, u32[]{:S(2)}) copy-start(bf16[128,768]{1,0:T(8,128)(2,1)} %param.8) | copy-start | bytes 589828
  350.5 9.7 %copy-start.72 = (f32[128]{0:T(128)S(1)}, f32[128]{0:T(128)}, u32[]{:S(2)}) copy-start(f32[128]{0:T(128)} %copy-done.71) | copy-start | bytes 1540
  350.5 9.9 %copy-start.95 = (f32[128]{0:T(128)S(1)}, f32[128]{0:T(128)}, u32[]{:S(2)}) copy-start(f32[128]{0:T(128)} %copy-done.94) | copy-start | bytes 1540
  350.5 9.9 %copy-start.85 = (f32[128]{0:T(128)S(1)}, f32[128]{0:T(128)}, u32[]{:S(2)}) copy-start(f32[128]{0:T(128)} %copy-done.84) | copy-start | bytes 1540
  351.2 9.5 %copy-start.34 = (f32[128,768]{1,0:T(8,128)S(1)}, f32[128,768]{1,0:T(8,128)}, u32[]{:S(2)}) copy-start(f32[128,768]{1,0:T(8,128)} %get-tuple-element.69) | copy-start | bytes 1179652
  351.2 9.5 %copy-start.36 = (f32[128,768]{1,0:T(8,128)S(1)}, f32[128,768]{1,0:T(8,128)}, u32[]{:S(2)}) copy-start(f32[128,768]{1,0:T(8,128)} %copy-done.35) | copy-start | bytes 1179652
  351.2 9.5 %copy-start.93 = (f32[128]{0:T(128)S(1)}, f32[128]{0:T(128)}, u32[]{:S(2)}) copy-start(f32[128]{0:T(128)} %copy-done.92) | copy-start | bytes 1540
  (74 other events, 231.3 us)
